TPU v7x, 512 devices: a whole 4x4x16 slice. The times are simulated.
512 devices in a mesh: dp: 16 (over z), tensor: 32 (over x, y, core).
Axes of the slice: x: 4, y: 4, z: 16, core: 2. Of those that a mesh axis runs over, the one named last changes fastest.
Arguments:
- context: bfloat16 [3072, 16384], P('tensor', 'dp'), may hold values from -6 to 6
- residual: bfloat16 [6144, 16384], P('tensor', 'dp'), may hold values from -110 to 110
- out_weight: bfloat16 [6144, 3072], P('tensor', 'dp'), may hold values from -0.109375 to 0.109375
- norm_gain: float32 [6144], P('tensor'), may hold values from 0.25 to 1.75
- norm_bias: float32 [6144], P('tensor'), may hold values from -4 to 4
- target: bfloat16 [6144, 16384], P('tensor', 'dp'), may hold values from -5 to 5
- probe: bfloat16 [6144, 3072], P('tensor'), may hold values from -1 to 1, as said below
Outputs:
- hess_diag: float32 [6144, 3072], P('tensor', 'dp')
- residual_grad: float32 [6144, 16384], P('tensor', 'dp')
Inputs may be any that keep to these rules, and one draw needn't show every extreme that they name: `probe`: every entry is -1 or +1.
All inputs are finite; a program needn't handle non-finite values.
Results may differ from a plain program's by a relative error of at most 0.0014.
Values may be sent and summed in bfloat16 or wider, within the bound.
A program may use at most 64 MiB of HBM per device.

v0:
```python
import jax
import jax.numpy as jnp
from jax import lax
from jax.sharding import PartitionSpec as P

D = 6144


def contract_tokens(left, right):
    return lax.dot_general(
        left, right, (((1,), (1,)), ((), ())), preferred_element_type=jnp.float32
    )


def shards(context, residual, out_weight, norm_gain, norm_bias, target, probe):
    weight = lax.all_gather(out_weight, "dp", axis=1, tiled=True)
    feat_count = weight.shape[0]
    stacked = jnp.concatenate([weight, probe], axis=0)
    whole_ctx = lax.all_gather(context, "tensor", axis=0, tiled=True)
    both_prod = jnp.dot(stacked, whole_ctx, preferred_element_type=jnp.float32)
    proj = both_prod[:feat_count]
    tangent = both_prod[feat_count:]
    gain = norm_gain[:, None]
    bias = norm_bias[:, None]
    resid = residual.astype(jnp.float32) + proj
    row_total = lax.psum(jnp.sum(resid, axis=0), "tensor")
    row_mean = (row_total / D)[None, :]
    cent = resid - row_mean
    row_var = lax.psum(jnp.sum(cent * cent, axis=0), "tensor") / D
    inv_scale = (1.0 / jnp.sqrt(row_var + 1e-05))[None, :]
    normed = cent * inv_scale
    grad_normed = gain * (gain * normed + bias - target.astype(jnp.float32))
    gain_sq = gain * gain
    sum_grad, sum_gradn, sum_tan, sum_tann = lax.psum(
        (
            jnp.sum(grad_normed, axis=0),
            jnp.sum(grad_normed * normed, axis=0),
            jnp.sum(tangent, axis=0),
            jnp.sum(normed * tangent, axis=0),
        ),
        "tensor",
    )
    grad_mean = (sum_grad / D)[None, :]
    grad_proj = (sum_gradn / D)[None, :]
    tan_mean = (sum_tan / D)[None, :]
    tan_proj = (sum_tann / D)[None, :]
    tan_normed = inv_scale * (tangent - tan_mean - normed * tan_proj)
    tan_grad = gain_sq * tan_normed
    sum_curv, sum_curvn = lax.psum(
        (jnp.sum(tan_grad, axis=0), jnp.sum(tan_grad * normed + grad_normed * tan_normed, axis=0)),
        "tensor",
    )
    curv_mean = (sum_curv / D)[None, :]
    curv_proj = (sum_curvn / D)[None, :]
    residual_grad = inv_scale * (grad_normed - grad_mean - normed * grad_proj)
    curvature = -inv_scale * tan_proj * residual_grad + inv_scale * (
        tan_grad - curv_mean - tan_normed * grad_proj - normed * curv_proj
    )
    curvature = curvature.astype(jnp.bfloat16)
    slice_cols = out_weight.shape[1]
    partial_value = contract_tokens(curvature, whole_ctx)
    summed = lax.psum_scatter(partial_value, "dp", scatter_dimension=1, tiled=True)
    col_offset = lax.axis_index("dp") * slice_cols
    probe_cols = lax.dynamic_slice_in_dim(probe, col_offset, slice_cols, 1)
    token_total = context.shape[1] * lax.axis_size("dp")
    hess_diag = probe_cols.astype(jnp.float32) * summed / token_total
    return (hess_diag, residual_grad)


def solution(mesh):
    return jax.shard_map(
        shards,
        mesh=mesh,
        in_specs=(
            P("tensor", "dp"),
            P("tensor", "dp"),
            P("tensor", "dp"),
            P("tensor"),
            P("tensor"),
            P("tensor", "dp"),
            P("tensor", None),
        ),
        out_specs=(P("tensor", "dp"), P("tensor", "dp")),
        check_vma=False,
    )
```

profile of v0, /device:TPU:1, one launch (start us, length us, event | category | flops | bytes accessed | tf_op | source)
XLA Modules:
  0.0 558.7 jit_solution(17074751844618398436)
XLA Ops:
  7.2 0.0 all-gather.3.cloned.1.call-start
  7.2 1.6 copy.9
  8.9 0.0 all-gather.3.cloned.1.call-update
  8.9 0.0 all-gather.5.cloned.1.call-start
  8.9 0.7 all-gather.5.cloned.1.call-update
  9.6 0.0 reduce-scatter.4.cloned.1.call-start
  9.7 1.6 copy.10
  11.3 0.0 copy-done.3
  11.4 0.0 copy-start.2
  11.4 67.2 %all-gather.3.cloned.1.call-done = bf16[192,3072]{0,1:T(8,128)(2,1)} async-done(((bf16[192,192]{0,1:T(8,128)(2,1)}), bf16[192,3072]{0,1:T(8,128)(2,1)}) %all-gather.3.cloned.1.call-update) | async-done | bytes 1179664 | tf_op jit(solution)/shard_map/all_gather | solution.py:16
  78.6 74.7 %all-gather.5.cloned.1.call-done = bf16[3072,1024]{1,0:T(8,128)(2,1)} async-done(((bf16[96,1024]{1,0:T(8,128)(2,1)}), bf16[3072,1024]{1,0:T(8,128)(2,1)}) %all-gather.5.cloned.1.call-update) | async-done | bytes 6291472 | tf_op jit(solution)/shard_map/all_gather | solution.py:19
  153.3 6.6 %fusion = f32[384,1024]{1,0:T(8,128)S(1)} fusion(bf16[3072,1024]{1,0:T(8,128)(2,1)} %all-gather.5.cloned.1.call-done, bf16[192,3072]{0,1:T(8,128)(2,1)S(1)} %copy.10, bf16[192,3072]{0,1:T(8,128)(2,1)} %all-gather.3.cloned.1.call-done), kind=kOutput, calls=%fused_computation.1 | convolution fusion | flops 2420637696 | bytes 10223616 | tf_op jit(solution)/shard_map/dot_general | solution.py:20
  159.9 0.0 copy-start
  159.9 0.0 copy-start.5
  160.0 0.1 fusion.12
  160.1 62.3 %psum.56 = f32[1024]{0:T(1024)S(1)} all-reduce(f32[1024]{0:T(1024)S(1)} %get-tuple-element.14), channel_id=1, replica_groups=mesh['dp'=16,'tensor'=32] {'tensor'}, use_global_device_ids=true, to_apply=%region_1.0 | all-reduce | flops 1024 | bytes 8192 | tf_op jit(solution)/shard_map/psum | solution.py:26
  222.4 0.1 multiply_reduce_fusion.2
  222.5 65.2 %psum.57 = f32[1024]{0:T(1024)S(1)} all-reduce(f32[1024]{0:T(1024)S(1)} %multiply_reduce_fusion.2), channel_id=1, replica_groups=mesh['dp'=16,'tensor'=32] {'tensor'}, use_global_device_ids=true, to_apply=%region_3.0 | all-reduce | flops 1024 | bytes 8192 | tf_op jit(solution)/shard_map/psum | solution.py:29
  287.7 0.2 slice_reduce_fusion
  287.9 63.7 %all-reduce.1 = (f32[1024]{0:T(1024)S(1)}, f32[1024]{0:T(1024)S(1)}) all-reduce(f32[1024]{0:T(1024)S(1)} %get-tuple-element.5, f32[1024]{0:T(1024)S(1)} %get-tuple-element.4), channel_id=1, replica_groups=mesh['dp'=16,'tensor'=32] {'tensor'}, use_global_device_ids=true, to_apply=%region_5.0 | all-reduce | flops 2048 | bytes 16384 | tf_op jit(solution)/shard_map/psum | solution.py:34
  351.6 0.6 negate_multiply_fusion
  352.2 0.6 copy-done.4
  352.8 0.6 multiply_reduce_fusion.3
  353.4 118.8 %all-reduce = (f32[1024]{0:T(1024)S(1)}, f32[1024]{0:T(1024)S(1)}, f32[1024]{0:T(1024)S(1)}, f32[1024]{0:T(1024)S(1)}) all-reduce(f32[1024]{0:T(1024)S(1)} %get-tuple-element.6, f32[1024]{0:T(1024)S(1)} %get-tuple-element.7, f32[1024]{0:T(1024)S(1)} %get-tuple-element.3, ...), channel_id=1, replica_groups=mesh['dp'=16,'tensor'=32] {'tensor'}, use_global_device_ids=true, to_apply=%region_9.0 | all-reduce | flops 4096 | bytes 32768 | tf_op jit(solution)/shard_map/psum | solution.py:34
  472.3 1.0 subtract_multiply_fusion.1
  473.3 0.0 copy-start.1
  473.3 7.0 %convolution_bitcast_fusion = f32[3072,192]{1,0:T(8,128)} fusion(bf16[3072,1024]{1,0:T(8,128)(2,1)} %all-gather.5.cloned.1.call-done, f32[192,1024]{1,0:T(8,128)S(1)} %subtract_multiply_fusion.1, f32[1024]{0:T(1024)S(1)} %broadcast_multiply_fusion, f32[1024]{0:T(1024)S(1)} %broadcast_multiply_fusion.1, f32[192]{0:T(256)} %copy-done.6, ...), kind=kOutput, calls=%fused_computation | convolution fusion | flops 1211105280 | bytes 11043584
  480.3 0.0 copy-done.1
  480.3 0.0 reduce-scatter.4.cloned.1.call-update
  480.4 69.1 %reduce-scatter.4.cloned.1.call-done = f32[192,192]{1,0:T(8,128)} async-done(((f32[3072,192]{1,0:T(8,128)}), f32[192,192]{1,0:T(8,128)}) %reduce-scatter.4.cloned.1.call-update) | async-done | bytes 147472
  549.4 1.0 copy.12
  550.5 1.7 multiply_multiply_fusion
  (14 shorter events, 0.0 us)
Async XLA Ops:
  7.2 4.2 copy-start.3
  7.2 71.4 %all-gather.3.cloned.1.call-start = ((), (), s32[]{:S(2)}) async-start(), calls=%async_computation.1 | async-start | bytes 1671168 | tf_op jit(solution)/shard_map/all_gather | solution.py:16
  8.9 144.4 %all-gather.5.cloned.1.call-start = ((), (), s32[]{:S(2)}) async-start(), calls=%async_computation.2 | async-start | bytes 6488064 | tf_op jit(solution)/shard_map/all_gather | solution.py:19
  9.6 539.8 %reduce-scatter.4.cloned.1.call-start = ((), (), s32[]{:S(2)}) async-start(), calls=%async_computation.3 | async-start | bytes 3342336
  11.4 340.8 %copy-start.6 = (f32[192]{0:T(256)}, f32[192]{0:T(256)S(1)}, u32[]{:S(2)}) copy-start(f32[192]{0:T(256)S(1)} %mul.130) | copy-start | bytes 2308
  11.4 148.6 %copy-start.2 = (bf16[192,1024]{1,0:T(8,128)(2,1)S(1)}, bf16[192,1024]{1,0:T(8,128)(2,1)}, u32[]{:S(2)}) copy-start(bf16[192,1024]{1,0:T(8,128)(2,1)} %param.8) | copy-start | bytes 1179652
  159.9 192.9 %copy-start = (bf16[192,1024]{1,0:T(8,128)(2,1)S(1)}, bf16[192,1024]{1,0:T(8,128)(2,1)}, u32[]{:S(2)}) copy-start(bf16[192,1024]{1,0:T(8,128)(2,1)} %param.12) | copy-start | bytes 1179652
  159.9 192.9 %copy-start.5 = (f32[192]{0:T(256)S(1)}, f32[192]{0:T(256)}, u32[]{:S(2)}) copy-start(f32[192]{0:T(256)} %param.11) | copy-start | bytes 2308
  352.2 0.6 copy-start.4
  473.3 7.0 %copy-start.1 = (f32[192,1024]{1,0:T(8,128)}, f32[192,1024]{1,0:T(8,128)S(1)}, u32[]{:S(2)}) copy-start(f32[192,1024]{1,0:T(8,128)S(1)} %subtract_multiply_fusion.1) | copy-start | bytes 2359300
Sparse Core Ops, SparseCore 0:
  10.7 67.9 all-gather.2
  81.7 71.5 all-gather.4
  480.5 68.8 reduce-scatter.3
where the time goes:
time: 568 us; the launch traced here: 559 us
  blocking collectives  310 us (55%)
  waiting for transfers between devices  212 us (37%)
  between operations  13.9 us (2%)
  matrix products  13.6 us (2%)
    psum x2, blocking collectives, shards(): lax.psum((jnp.sum(grad_normed, axis=0), jnp.sum(grad_normed * normed, axi...  182 us
    all_gather x1, waiting for transfers between devices, shards(): whole_ctx = lax.all_gather(context, 'tensor', axis=0, tiled=True)  74.7 us
    unnamed x4, waiting for transfers between devices  69.8 us
    all_gather x1, waiting for transfers between devices, shards(): weight = lax.all_gather(out_weight, 'dp', axis=1, tiled=True)  67.2 us
    psum x1, blocking collectives, shards(): row_var = lax.psum(jnp.sum(cent * cent, axis=0), 'tensor') / D  65.2 us
    psum x1, blocking collectives, shards(): row_total = lax.psum(jnp.sum(resid, axis=0), 'tensor')  62.3 us
  transfers between devices with their start and end apart: 3, of which 3 were waited for; matrix products, arithmetic and copies ran while one was open for 0% of the time, Pallas kernels for 0%

commit v1 on v0

v1 whole, which is shorter than its diff:
```python
import jax
import jax.numpy as jnp
from jax import lax
from jax.experimental import pallas as pl
from jax.experimental.pallas import tpu as pltpu
from jax.sharding import PartitionSpec as P

MESH = pl.DeviceIdType.MESH
F32 = jnp.float32
BF16 = jnp.bfloat16

D = 6144
ROWS = 192
TOK = 1024
BLK = 96
NZ = 16
NT = 32
PK = 288
SUB = 144
TOKENS = 16384


def kernel(
    ctx_in, res_in, w_in, gain_ref, bias_ref, tgt_in, probe_in,
    hess_ref, rg_out,
    ctx, stk, pk, wloc, probe, res, tgt, xv, tau, gainb, biasb, mom, mbuf, cbuf, curv, curvt, rg, rs,
    load_sem, ctx_send, p_recv, q_recv, c_recv, pk_send, pkr_recv, pkl_recv,
    mom_send, mom_recv, cf_send, cf_recv, rs_send, rsr_recv, rsl_recv,
):
    z = lax.axis_index("dp")
    t = lax.axis_index("tensor")
    core = lax.rem(t, 2)
    x = lax.div(t, 8)
    y = lax.rem(lax.div(t, 2), 4)
    p = x + core * (y - x)
    q = y + core * (x - y)
    sp = 8 - 6 * core
    sq = 2 + 6 * core

    def dev(dp, dq):
        return lax.rem(p + dp + 4, 4) * sp + lax.rem(q + dq + 4, 4) * sq + core

    other = t + 1 - 2 * core
    z_up = lax.rem(z + 1, NZ)
    z_down = lax.rem(z + NZ - 1, NZ)

    def wait_bytes(ref, sem):
        pltpu.make_async_copy(ref, ref, sem).wait()

    def send(src, dst, ssem, rsem, zz, tt):
        pltpu.make_async_remote_copy(
            src_ref=src, dst_ref=dst, send_sem=ssem, recv_sem=rsem, device_id=(zz, tt), device_id_type=MESH
        ).start()

    own_rows = pl.ds(pl.multiple_of(t * BLK, 32), BLK)
    loads = [
        pltpu.make_async_copy(w_in, wloc, load_sem.at[0]),
        pltpu.make_async_copy(probe_in, probe, load_sem.at[1]),
        pltpu.make_async_copy(ctx_in, ctx.at[own_rows, :], load_sem.at[2]),
        pltpu.make_async_copy(res_in, res, load_sem.at[3]),
        pltpu.make_async_copy(tgt_in, tgt, load_sem.at[4]),
    ]
    for c in loads:
        c.start()

    barrier = pltpu.get_barrier_semaphore()
    for zz in (z_up, z_down):
        pl.semaphore_signal(barrier, inc=1, device_id=(zz, t), device_id_type=MESH)

    def greet(i, carry):
        pl.semaphore_signal(barrier, inc=1, device_id=(z, lax.rem(t + i, NT)), device_id_type=MESH)
        return carry

    lax.fori_loop(1, NT, greet, 0)
    pl.semaphore_wait(barrier, NT + 1)

    def rows_of(dp, dq):
        return pl.ds(pl.multiple_of(dev(dp, dq) * BLK, 32), BLK)

    def blk(dp, dq, half=None):
        if half is None:
            return ctx.at[rows_of(dp, dq), :]
        return ctx.at[rows_of(dp, dq), pl.ds(half * 512, 512)]

    def to_core(dp, dq, src=None):
        b = blk(dp, dq)
        send(b if src is None else src, b, ctx_send, c_recv.at[(dp % 4) * 4 + dq % 4], z, other)

    def along_q(dp, src=None):
        b = blk(dp, 0)
        s = b if src is None else src
        send(s, b, ctx_send, q_recv.at[(dp % 4) * 4 + 0], z, dev(0, 1))
        send(s, b, ctx_send, q_recv.at[(dp % 4) * 4 + 1], z, dev(0, -1))

    own = ctx.at[own_rows, :]
    send(ctx_in, own, ctx_send, p_recv.at[0], z, dev(1, 0))
    send(ctx_in, own, ctx_send, p_recv.at[1], z, dev(-1, 0))
    along_q(0, ctx_in)
    to_core(0, 0, ctx_in)

    def pk_sub(j, s):
        return pk.at[j, pl.ds(s * SUB, SUB), :]

    def pk_send_to(j, s, up, step):
        ref = pk_sub(j, s)
        if up:
            send(ref, ref, pk_send, pkr_recv.at[step * 2 + s], z_up, t)
        else:
            send(ref, ref, pk_send, pkl_recv.at[step * 2 + s], z_down, t)

    loads[0].wait()
    pk[z, 0:192, :] = wloc[:, 0:128]
    pk[z, 192:288, 0:64] = wloc[0:96, 128:192]
    pk[z, 192:288, 64:128] = wloc[96:192, 128:192]
    for s in range(2):
        pk_send_to(z, s, True, 0)
        pk_send_to(z, s, False, 0)

    def unpack(j):
        stk[j, 0:192, 0:128] = pk[j, 0:192, :]
        stk[j, 0:96, 128:192] = pk[j, 192:288, 0:64]
        stk[j, 96:192, 128:192] = pk[j, 192:288, 64:128]

    def z_step(n):
        below = lax.rem(z + NZ - n, NZ)
        above = lax.rem(z + n, NZ)
        for s in range(2):
            if n < 8 or s == 0:
                wait_bytes(pk_sub(below, s), pkr_recv.at[(n - 1) * 2 + s])
                if n < 7 or (n == 7 and s == 0):
                    pk_send_to(below, s, True, n)
            if n < 8 or s == 1:
                wait_bytes(pk_sub(above, s), pkl_recv.at[(n - 1) * 2 + s])
                if n < 7 or (n == 7 and s == 1):
                    pk_send_to(above, s, False, n)
        unpack(below)
        if n < 8:
            unpack(above)

    unpack(z)
    loads[1].wait()
    for j in range(NZ):
        stk[j, 192:384, :] = probe[:, 192 * j : 192 * (j + 1)]
    gainb[...] = jnp.transpose(jnp.broadcast_to(gain_ref[...], (128, ROWS)))
    biasb[...] = jnp.transpose(jnp.broadcast_to(bias_ref[...], (128, ROWS)))

    def take_p(dp):
        wait_bytes(blk(dp, 0), p_recv.at[0 if dp < 0 else 1])
        half = 0 if dp < 0 else 1
        b = blk(dp, 0, half)
        send(b, b, ctx_send, p_recv.at[2 + half], z, dev(-dp, 0))
        along_q(dp)
        to_core(dp, 0)

    def take_p2():
        for half in range(2):
            wait_bytes(blk(2, 0, half), p_recv.at[2 + half])
        along_q(2)
        to_core(2, 0)

    def take_q(dp):
        for dq in (-1, 1):
            half = 0 if dq < 0 else 1
            wait_bytes(blk(dp, dq), q_recv.at[(dp % 4) * 4 + half])
            b = blk(dp, dq, half)
            send(b, b, ctx_send, q_recv.at[(dp % 4) * 4 + 2 + half], z, dev(0, -dq))
            to_core(dp, dq)

    def take_q2(dp):
        for half in range(2):
            wait_bytes(blk(dp, 2, half), q_recv.at[(dp % 4) * 4 + 2 + half])
        to_core(dp, 2)

    take_p(-1)
    take_p(1)
    z_step(1)
    take_q(0)
    take_p2()
    z_step(2)
    take_q(-1)
    z_step(3)
    take_q(1)
    z_step(4)
    take_q2(0)
    take_q(2)
    z_step(5)
    take_q2(-1)
    z_step(6)
    take_q2(1)
    z_step(7)
    take_q2(2)
    z_step(8)
    for c in loads[2:]:
        c.wait()

    def other_rows(dp, dq):
        osp = 2 + 6 * core
        osq = 8 - 6 * core
        o = lax.rem(q + dp + 4, 4) * osp + lax.rem(p + dq + 4, 4) * osq + 1 - core
        return ctx.at[pl.ds(pl.multiple_of(o * BLK, 32), BLK), :]

    for dp in range(4):
        for dq in range(4):
            wait_bytes(other_rows(dp, dq), c_recv.at[dp * 4 + dq])

    for n in range(4):
        cols = slice(n * 256, (n + 1) * 256)

        def add(j, carry):
            rows = pl.ds(pl.multiple_of(j * 192, 64), 192)
            return carry + jnp.dot(stk[j], ctx[rows, cols], preferred_element_type=F32)

        both = lax.fori_loop(0, NZ, add, jnp.zeros((384, 256), F32))
        xv[:, cols] = both[0:192]
        tau[:, cols] = both[192:384]

    def sums(k, carry):
        lanes = pl.ds(pl.multiple_of(k * 128, 128), 128)
        tot = jnp.zeros((16, 128), F32)
        for r in range(12):
            rows = pl.ds(r * 16, 16)
            xx = xv[rows, lanes] + res[rows, lanes].astype(F32)
            xv[rows, lanes] = xx
            tot = tot + xx
        mean = jnp.sum(tot, axis=0, keepdims=True) / ROWS
        accs = [jnp.zeros((16, 128), F32) for _ in range(11)]
        for r in range(12):
            rows = pl.ds(r * 16, 16)
            yy = xv[rows, lanes] - mean
            tt = tau[rows, lanes]
            g = gainb[rows, :]
            w = g * g
            h = g * (biasb[rows, :] - tgt[rows, lanes].astype(F32))
            wy = w * yy
            wt = w * tt
            terms = (yy * yy, wy, wy * yy, h, h * yy, tt, yy * tt, wt, wy * tt, h * tt, w)
            accs = [a + b for a, b in zip(accs, terms)]
        mom[k, 0:1, :] = mean
        for i in range(11):
            mom[k, i + 1 : i + 2, :] = jnp.sum(accs[i], axis=0, keepdims=True)
        return carry

    mom[...] = jnp.zeros((8, 16, 128), F32)
    lax.fori_loop(0, 8, sums, 0)

    mine = lax.div(t, 4)
    is_owner = lax.rem(t, 4) == 0
    for k in range(8):

        @pl.when(t != 4 * k)
        def _():
            send(mom.at[k], mbuf.at[t], mom_send, mom_recv, z, 4 * k)

    @pl.when(is_owner)
    def _():
        mbuf[t] = mom[mine]
        wait_bytes(mbuf.at[pl.ds(0, NT - 1)], mom_recv)
        (mi, yy, wy, wyy, h, hy, tt, yt, wt, wyt, ht, w) = [mbuf[:, i, :] for i in range(12)]

        def total(a):
            return jnp.sum(a, axis=0, keepdims=True)

        mean = total(mi) / NT
        d = mi - mean
        s_zz = total(yy + ROWS * d * d)
        s_wz = total(wy + d * w)
        s_wzz = total(wyy + d * (2 * wy + d * w))
        s_h = total(h)
        s_hz = total(hy + d * h)
        s_t = total(tt)
        s_zt = total(yt + d * tt)
        s_wt = total(wt)
        s_wzt = total(wyt + d * wt)
        s_ht = total(ht)
        s_w = total(w)
        sc = 1.0 / jnp.sqrt(s_zz / D + 1e-05)
        s_wn = sc * s_wz
        s_wnn = sc * sc * s_wzz
        s_hn = sc * s_hz
        g_mean = (s_wn + s_h) / D
        g_proj = (s_wnn + s_hn) / D
        t_mean = s_t / D
        t_proj = sc * s_zt / D
        c_mean = sc * (s_wt - t_mean * s_w - t_proj * s_wn) / D
        c_proj = sc * (2 * (sc * s_wzt - t_mean * s_wn - t_proj * s_wnn) + s_ht - t_mean * s_h - t_proj * s_hn) / D
        for i, v in enumerate((mean, sc, g_mean, g_proj, t_mean, t_proj, c_mean, c_proj)):
            cbuf[mine, i : i + 1, :] = v

        def tell(i, carry):
            send(cbuf.at[mine], cbuf.at[mine], cf_send, cf_recv.at[mine], z, lax.rem(t + i, NT))
            return carry

        lax.fori_loop(1, NT, tell, 0)

    for k in range(8):

        @pl.when(t != 4 * k)
        def _():
            wait_bytes(cbuf.at[k], cf_recv.at[k])

    def finish(k, carry):
        lanes = pl.ds(pl.multiple_of(k * 128, 128), 128)
        mean, sc, g_mean, g_proj, t_mean, t_proj, c_mean, c_proj = [cbuf[k, i : i + 1, :] for i in range(8)]
        lead = -sc * t_proj
        for r in range(12):
            rows = pl.ds(r * 16, 16)
            n = (xv[rows, lanes] - mean) * sc
            g = gainb[rows, :]
            w = g * g
            gn = g * (g * n + biasb[rows, :] - tgt[rows, lanes].astype(F32))
            grad = sc * (gn - g_mean - n * g_proj)
            rg[rows, lanes] = grad
            u = sc * (tau[rows, lanes] - t_mean - n * t_proj)
            cv = lead * grad + sc * (w * u - c_mean - u * g_proj - n * c_proj)
            curv[rows, :] = cv
            if r >= 8:
                curv[pl.ds(r * 16 + 64, 16), :] = cv
        curvt[pl.ds(pl.multiple_of(k * 128, 128), 128), :] = jnp.transpose(curv[...]).astype(BF16)
        return carry

    lax.fori_loop(0, 8, finish, 0)
    rg_copy = pltpu.make_async_copy(rg, rg_out, load_sem.at[5])
    rg_copy.start()

    rsr = rs.at[pl.ds(0, 9)]
    rsl = rs.at[pl.ds(9, 9)]

    def product(j):
        rows = pl.ds(pl.multiple_of(j * 192, 64), 192)
        full = jnp.dot(ctx[rows, :], curvt[...], preferred_element_type=F32)
        lane = lax.broadcasted_iota(jnp.int32, (96, 128), 1)
        return full[:, 0:128], jnp.where(lane < 64, full[0:96, 128:256], full[96:192, 128:256])

    def put(buf, n, j, add):
        a, b = product(j)
        if add:
            buf[n, 0:192, :] = buf[n, 0:192, :] + a
            buf[n, 192:288, :] = buf[n, 192:288, :] + b
        else:
            buf[n, 0:192, :] = a
            buf[n, 192:288, :] = b

    def rs_send_to(buf, n, s, up):
        src = buf.at[n, pl.ds(s * SUB, SUB), :]
        dst = buf.at[n + 1, pl.ds(s * SUB, SUB), :]
        if up:
            send(src, dst, rs_send, rsr_recv.at[n * 2 + s], z_up, t)
        else:
            send(src, dst, rs_send, rsl_recv.at[n * 2 + s], z_down, t)

    far = lax.rem(z + 8, NZ)
    put(rsr, 0, far, False)
    rs_send_to(rsr, 0, 0, True)
    src = rsr.at[0, pl.ds(SUB, SUB), :]
    send(src, rsl.at[1, pl.ds(SUB, SUB), :], rs_send, rsl_recv.at[1], z_down, t)
    for n in range(1, 8):
        for up in (True, False):
            buf, sem = (rsr, rsr_recv) if up else (rsl, rsl_recv)
            j = lax.rem(z + 8 - n, NZ) if up else lax.rem(z + 8 + n, NZ)
            a, b = product(j)
            if n == 1:
                s = 0 if up else 1
                wait_bytes(buf.at[n, pl.ds(s * SUB, SUB), :], sem.at[(n - 1) * 2 + s])
                lo = 0 if up else SUB
                whole = jnp.concatenate([a, b], axis=0)
                buf[n, lo : lo + SUB, :] = buf[n, lo : lo + SUB, :] + whole[lo : lo + SUB]
                rs_send_to(buf, n, s, up)
                buf[n, SUB - lo : 2 * SUB - lo, :] = whole[SUB - lo : 2 * SUB - lo]
                rs_send_to(buf, n, 1 - s, up)
            else:
                whole = jnp.concatenate([a, b], axis=0)
                for s in range(2):
                    lo = s * SUB
                    wait_bytes(buf.at[n, pl.ds(lo, SUB), :], sem.at[(n - 1) * 2 + s])
                    buf[n, lo : lo + SUB, :] = buf[n, lo : lo + SUB, :] + whole[lo : lo + SUB]
                    rs_send_to(buf, n, s, up)
    a, b = product(z)
    for s in range(2):
        wait_bytes(rsr.at[8, pl.ds(s * SUB, SUB), :], rsr_recv.at[14 + s])
        wait_bytes(rsl.at[8, pl.ds(s * SUB, SUB), :], rsl_recv.at[14 + s])
    a = a + rsr[8, 0:192, :] + rsl[8, 0:192, :]
    b = b + rsr[8, 192:288, :] + rsl[8, 192:288, :]
    at = jnp.transpose(a)
    bt = jnp.transpose(b)
    pc = stk[z, 192:384, :].astype(F32)
    hess_ref[0:128, :] = pc[0:128] * at / TOKENS
    hess_ref[128:192, 0:96] = pc[128:192, 0:96] * bt[0:64] / TOKENS
    hess_ref[128:192, 96:192] = pc[128:192, 96:192] * bt[64:128] / TOKENS

    rg_copy.wait()
    wait_bytes(ctx.at[pl.ds(0, 31 * BLK), :], ctx_send)
    wait_bytes(pk.at[pl.ds(0, 15)], pk_send)
    wait_bytes(rs.at[pl.ds(0, 15)], rs_send)

    @pl.when(is_owner)
    def _():
        wait_bytes(mom.at[pl.ds(0, 7)], mom_send)
        wait_bytes(rs.at[0, pl.ds(0, 8 * (NT - 1)), :], cf_send)

    @pl.when(jnp.logical_not(is_owner))
    def _():
        wait_bytes(mom, mom_send)


def shards(context, residual, out_weight, norm_gain, norm_bias, target, probe):
    hbm = pl.BlockSpec(memory_space=pl.ANY)
    vmem = pl.BlockSpec(memory_space=pltpu.VMEM)
    dma = pltpu.SemaphoreType.DMA
    return pl.pallas_call(
        kernel,
        out_shape=(
            jax.ShapeDtypeStruct((ROWS, 192), F32),
            jax.ShapeDtypeStruct((ROWS, TOK), F32),
        ),
        in_specs=[hbm, hbm, hbm, vmem, vmem, hbm, hbm],
        out_specs=(vmem, hbm),
        scratch_shapes=[
            pltpu.VMEM((NT * BLK, TOK), BF16),
            pltpu.VMEM((NZ, 384, 192), BF16),
            pltpu.VMEM((NZ, PK, 128), BF16),
            pltpu.VMEM((192, 192), BF16),
            pltpu.VMEM((ROWS, 3072), BF16),
            pltpu.VMEM((ROWS, TOK), BF16),
            pltpu.VMEM((ROWS, TOK), BF16),
            pltpu.VMEM((ROWS, TOK), F32),
            pltpu.VMEM((ROWS, TOK), F32),
            pltpu.VMEM((ROWS, 128), F32),
            pltpu.VMEM((ROWS, 128), F32),
            pltpu.VMEM((8, 16, 128), F32),
            pltpu.VMEM((NT, 16, 128), F32),
            pltpu.VMEM((8, 8, 128), F32),
            pltpu.VMEM((256, 128), F32),
            pltpu.VMEM((TOK, 256), BF16),
            pltpu.VMEM((ROWS, TOK), F32),
            pltpu.VMEM((18, PK, 128), F32),
            dma((6,)),
            dma,
            dma((4,)),
            dma((16,)),
            dma((16,)),
            dma,
            dma((16,)),
            dma((16,)),
            dma,
            dma,
            dma,
            dma((8,)),
            dma,
            dma((16,)),
            dma((16,)),
        ],
        compiler_params=pltpu.CompilerParams(
            collective_id=0, has_side_effects=True, vmem_limit_bytes=48 * 1024 * 1024
        ),
    )(context, residual, out_weight, norm_gain.reshape(1, ROWS), norm_bias.reshape(1, ROWS), target, probe)


def solution(mesh):
    return jax.shard_map(
        shards,
        mesh=mesh,
        in_specs=(
            P("tensor", "dp"),
            P("tensor", "dp"),
            P("tensor", "dp"),
            P("tensor"),
            P("tensor"),
            P("tensor", "dp"),
            P("tensor", None),
        ),
        out_specs=(P("tensor", "dp"), P("tensor", "dp")),
        check_vma=False,
    )
```

time: 568 us -> 120 us (0.21)
  the two profiles are of different devices: /device:TPU:1 before, /device:TPU:4 now
where the time goes in v1:
time: 120 us; the launch traced here: 119 us
  Pallas kernels  111 us (92%)
  local copies, waits for them, and re-layouts  7.99 us (7%)
    pallas_call x1, Pallas kernels, shards(): pl.pallas_call(kernel, out_shape=(jax.ShapeDtypeStruct((ROWS, 192), F32),...  111 us
    unnamed x16, local copies, waits for them, and re-layouts  7.99 us

profile of v1, /device:TPU:4, one launch (start us, length us, event | category | flops | bytes accessed | tf_op | source)
XLA Modules:
  0.0 119.5 jit_solution(11863301766271597029)
XLA Ops:
  0.6 0.0 copy-start
  0.6 1.3 %copy-done = bf16[192,3072]{1,0:T(8,128)(2,1)S(1)} copy-done((bf16[192,3072]{1,0:T(8,128)(2,1)S(1)}, bf16[192,3072]{1,0:T(8,128)(2,1)}, u32[]{:S(2)}) %copy-start) | copy-done | bytes 1179672
  1.9 0.0 copy-start.1
  1.9 1.0 copy-done.1
  2.9 0.0 copy-start.2
  2.9 1.0 copy-done.2
  3.9 0.0 copy-start.3
  3.9 0.9 copy-done.3
  4.8 0.0 copy-start.4
  4.8 0.9 copy-done.4
  5.7 0.0 copy-start.5
  5.7 0.7 copy-done.5
  6.4 0.0 copy-start.6
  6.4 0.7 copy-done.6
  7.1 110.9 %shard_map.86 = (f32[192,192]{1,0:T(8,128)S(1)}, f32[192,1024]{1,0:T(8,128)S(1)}) custom-call(bf16[96,1024]{1,0:T(8,128)(2,1)S(1)} %copy-done.3, bf16[192,1024]{1,0:T(8,128)(2,1)S(1)} %copy-done.1, bf16[192,192]{1,0:T(8,128)(2,1)S(1)} %copy-done.4, f32[1,192]{1,0:T(1,128)S(1)} %bitcast.2, f32[1,192]{1,0:T(1,128)S(1)} %bitcast.3, ...), custom_call_target="tpu_custom_call" | custom-call | tf_op jit(solution)/shard_map/pallas_call | solution.py:409
  117.9 0.7 copy.11
  118.6 0.9 copy.12
Async XLA Ops:
  0.6 1.3 %copy-start = (bf16[192,3072]{1,0:T(8,128)(2,1)S(1)}, bf16[192,3072]{1,0:T(8,128)(2,1)}, u32[]{:S(2)}) copy-start(bf16[192,3072]{1,0:T(8,128)(2,1)} %probe_in.1) | copy-start | bytes 3538948
  1.9 1.0 copy-start.1
  2.9 1.0 copy-start.2
  3.9 0.9 copy-start.3
  4.8 0.9 copy-start.4
  5.7 0.7 copy-start.5
  6.4 0.7 copy-start.6

commit v2 on v1

v2 whole, which is shorter than its diff:
```python
import jax
import jax.numpy as jnp
from jax import lax
from jax.experimental import pallas as pl
from jax.experimental.pallas import tpu as pltpu
from jax.sharding import PartitionSpec as P

MESH = pl.DeviceIdType.MESH
F32 = jnp.float32
BF16 = jnp.bfloat16

D = 6144
ROWS = 192
TOK = 1024
BLK = 96
NZ = 16
NT = 32
PK = 288
SUB = 144
TOKENS = 16384

PLAN = (
    ("S", "p", 1), ("S", "p", -1), ("S", "zu", 1, 0), ("S", "zd", 1, 1), ("S", "zd", 1, 0), ("S", "zu", 1, 1),
    ("W", "zu", 1, 0), ("S", "zu", 2, 0), ("S", "q", 0, -1), ("S", "q", 0, 1), ("W", "zd", 1, 1), ("S", "zd", 2, 1),
    ("W", "zd", 1, 0), ("W", "zu", 1, 1), ("W", "p", 1), ("S", "zu", 2, 1), ("W", "p", -1), ("S", "p2", 1),
    ("S", "zd", 2, 0), ("W", "zu", 2, 0), ("S", "zu", 3, 0), ("S", "q", -1, -1), ("W", "zd", 2, 1), ("S", "zd", 3, 1),
    ("W", "zu", 2, 1), ("W", "zd", 2, 0), ("S", "zu", 3, 1), ("S", "q", 1, 1), ("S", "zd", 3, 0), ("S", "p2", 0),
    ("W", "zu", 3, 0), ("S", "zu", 4, 0), ("W", "zd", 3, 1), ("S", "zd", 4, 1), ("W", "zu", 3, 1), ("S", "zu", 4, 1),
    ("S", "q", 1, -1), ("W", "p2", 1), ("W", "zd", 3, 0), ("S", "q", -1, 1), ("S", "zd", 4, 0), ("W", "zu", 4, 0),
    ("S", "zu", 5, 0), ("W", "zd", 4, 1), ("S", "zd", 5, 1), ("W", "q", 1, 1), ("W", "p2", 0), ("W", "q", -1, -1),
    ("S", "q2h", 0, 1), ("W", "zu", 4, 1), ("S", "q2h", 1, 1), ("S", "zu", 5, 1), ("S", "q2h", 0, -1),
    ("S", "qq", -1, 0), ("W", "q", 0, 1), ("W", "zd", 4, 0), ("S", "zd", 5, 0), ("W", "zu", 5, 0), ("S", "zu", 6, 0),
    ("S", "q2h", 1, -1), ("W", "zd", 5, 1), ("S", "zd", 6, 1), ("W", "zu", 5, 1), ("S", "qq", 1, 1),
    ("S", "qq", 0, 1), ("S", "zu", 6, 1), ("W", "zd", 5, 0), ("W", "q", 0, -1), ("S", "zd", 6, 0), ("S", "qq", 0, 0),
    ("W", "zu", 6, 0), ("S", "zu", 7, 0), ("W", "q", 1, -1), ("W", "zd", 6, 1), ("S", "zd", 7, 1), ("W", "q", -1, 1),
    ("S", "qq", 1, 0), ("S", "qq", -1, 1), ("W", "zd", 6, 0), ("W", "q2h", 1, 1), ("W", "zu", 6, 1),
    ("W", "q2h", 0, -1), ("S", "zd", 7, 0), ("S", "zu", 7, 1), ("S", "qq", 2, 0), ("S", "qq", 2, 1),
    ("W", "zu", 7, 0), ("S", "zu", 8, 0), ("W", "zd", 7, 1), ("S", "zd", 8, 1), ("W", "qq", 1, 1),
    ("W", "q2h", 1, -1), ("W", "qq", -1, 1), ("W", "qq", -1, 0), ("W", "qq", 0, 1), ("W", "zu", 7, 1),
    ("W", "zd", 7, 0), ("W", "qq", 0, 0), ("W", "q2h", 0, 1), ("W", "qq", 1, 0), ("W", "zu", 8, 0), ("W", "qq", 2, 0),
    ("W", "qq", 2, 1), ("W", "zd", 8, 1),
)

def kernel(
    ctx_in, res_in, w_in, gain_in, bias_in, tgt_in, probe_in,
    hess_ref, rg_out,
    ctx, stk, pk, wloc, res, tgt, xv, tau, grow, brow, gainb, biasb, mom, mbuf, cbuf, curv, curvt, rg, rs, prod,
    load_sem, ctx_send, p_recv, q_recv, c_recv, pk_send, pkr_recv, pkl_recv,
    mom_send, mom_recv, cf_send, cf_recv, rs_send, rsr_recv, rsl_recv,
):
    z = lax.axis_index("dp")
    t = lax.axis_index("tensor")
    core = lax.rem(t, 2)
    x = lax.div(t, 8)
    y = lax.rem(lax.div(t, 2), 4)
    p = x + core * (y - x)
    q = y + core * (x - y)
    sp = 8 - 6 * core
    sq = 2 + 6 * core

    def dev(dp, dq):
        return lax.rem(p + dp + 4, 4) * sp + lax.rem(q + dq + 4, 4) * sq + core

    other = t + 1 - 2 * core
    z_up = lax.rem(z + 1, NZ)
    z_down = lax.rem(z + NZ - 1, NZ)

    def wait_bytes(ref, sem):
        pltpu.make_async_copy(ref, ref, sem).wait()

    def send(src, dst, ssem, rsem, zz, tt):
        pltpu.make_async_remote_copy(
            src_ref=src, dst_ref=dst, send_sem=ssem, recv_sem=rsem, device_id=(zz, tt), device_id_type=MESH
        ).start()

    barrier = pltpu.get_barrier_semaphore()
    for zz in (z_up, z_down):
        pl.semaphore_signal(barrier, inc=1, device_id=(zz, t), device_id_type=MESH)

    def greet(i, carry):
        pl.semaphore_signal(barrier, inc=1, device_id=(z, lax.rem(t + i, NT)), device_id_type=MESH)
        return carry

    lax.fori_loop(1, NT, greet, 0)

    own_rows = pl.ds(pl.multiple_of(t * BLK, 32), BLK)
    own = ctx.at[own_rows, :]
    loads = [
        pltpu.make_async_copy(w_in, wloc, load_sem.at[0]),
        pltpu.make_async_copy(probe_in, stk.at[pl.ds(ROWS, ROWS), :], load_sem.at[1]),
        pltpu.make_async_copy(ctx_in, own, load_sem.at[2]),
        pltpu.make_async_copy(res_in, res, load_sem.at[3]),
        pltpu.make_async_copy(tgt_in, tgt, load_sem.at[4]),
        pltpu.make_async_copy(gain_in, grow, load_sem.at[6]),
        pltpu.make_async_copy(bias_in, brow, load_sem.at[7]),
    ]
    for c in loads:
        c.start()
    loads[0].wait()
    pk[z, 0:192, :] = wloc[:, 0:128]
    pk[z, 192:288, 0:64] = wloc[0:96, 128:192]
    pk[z, 192:288, 64:128] = wloc[96:192, 128:192]
    pl.semaphore_wait(barrier, NT + 1)

    def blk(dp, dq, half=None):
        rows = pl.ds(pl.multiple_of(dev(dp, dq) * BLK, 32), BLK)
        if half is None:
            return ctx.at[rows, :]
        return ctx.at[rows, pl.ds(half * 512, 512)]

    def to_core(dp, dq, src=None):
        b = blk(dp, dq)
        send(b if src is None else src, b, ctx_send, c_recv.at[(dp % 4) * 4 + dq % 4], z, other)

    def route(kind, a, b=None):
        if kind == "p":
            return blk(a, 0), p_recv.at[0 if a < 0 else 1], (0, 0, None), (-a, 0)
        if kind == "p2":
            d = -1 if a == 0 else 1
            return blk(2, 0, a), p_recv.at[2 + a], (d, 0, a), (-d, 0)
        if kind == "q":
            return blk(a, b), q_recv.at[(a % 4) * 6 + (0 if b < 0 else 1)], (a, 0, None), (0, -b)
        if kind == "q2h":
            return blk(2, b, a), q_recv.at[12 + (0 if b < 0 else 1) + 2 * a], (2, 0, a), (0, -b)
        d = -1 if b == 0 else 1
        return blk(a, 2, b), q_recv.at[(a % 4) * 6 + 4 + b], (a, d, b), (0, -d)

    def pk_sub(j, s):
        return pk.at[j, pl.ds(s * SUB, SUB), :]

    def z_block(up, n):
        return lax.rem(z + NZ - n, NZ) if up else lax.rem(z + n, NZ)

    arrived = set()
    for act, kind, *ab in PLAN:
        if kind in ("zu", "zd"):
            n, s = ab
            up = kind == "zu"
            sem = (pkr_recv if up else pkl_recv).at[(n - 1) * 2 + s]
            if act == "S":
                ref = pk_sub(z_block(up, n - 1), s)
                send(ref, ref, pk_send, sem, z_up if up else z_down, t)
            else:
                wait_bytes(pk_sub(z_block(up, n), s), sem)
            continue
        dst, sem, (dp, dq, half), to = route(kind, *ab)
        if act == "S":
            src = blk(dp, dq, half)
            if (dp, dq) == (0, 0):
                send(ctx_in, src, ctx_send, sem, z, dev(*to))
                if kind == "q" and ab[1] == 1:
                    to_core(0, 0, ctx_in)
            else:
                send(src, src, ctx_send, sem, z, dev(*to))
            continue
        wait_bytes(dst, sem)
        arrived.add((kind, *ab))
        if kind == "p":
            to_core(ab[0], 0)
        elif kind == "q":
            to_core(*ab)
        elif kind == "p2" and ("p2", 1 - ab[0]) in arrived:
            to_core(2, 0)
        elif kind == "q2h" and ("q2h", 1 - ab[0], ab[1]) in arrived:
            to_core(2, ab[1])
        elif kind == "qq" and ("qq", ab[0], 1 - ab[1]) in arrived:
            to_core(ab[0], 2)

    for c in loads[5:]:
        c.wait()
    gainb[...] = jnp.transpose(jnp.broadcast_to(grow[...], (128, ROWS)))
    biasb[...] = jnp.transpose(jnp.broadcast_to(brow[...], (128, ROWS)))
    for j in range(NZ):
        c = 192 * j
        stk[0:192, c : c + 128] = pk[j, 0:192, :]
        stk[0:96, c + 128 : c + 192] = pk[j, 192:288, 0:64]
        stk[96:192, c + 128 : c + 192] = pk[j, 192:288, 64:128]

    for c in loads[1:5]:
        c.wait()

    def other_rows(dp, dq):
        osp = 2 + 6 * core
        osq = 8 - 6 * core
        o = lax.rem(q + dp + 4, 4) * osp + lax.rem(p + dq + 4, 4) * osq + 1 - core
        return ctx.at[pl.ds(pl.multiple_of(o * BLK, 32), BLK), :]

    for dp in range(4):
        for dq in range(4):
            wait_bytes(other_rows(dp, dq), c_recv.at[dp * 4 + dq])

    for n in range(2):
        cols = slice(n * 512, (n + 1) * 512)
        both = jnp.dot(stk[...], ctx[:, cols], preferred_element_type=F32)
        xv[:, cols] = both[0:192]
        tau[:, cols] = both[192:384]

    def sums(k, carry):
        lanes = pl.ds(pl.multiple_of(k * 128, 128), 128)
        tot = jnp.zeros((16, 128), F32)
        for r in range(12):
            rows = pl.ds(r * 16, 16)
            xx = xv[rows, lanes] + res[rows, lanes].astype(F32)
            xv[rows, lanes] = xx
            tot = tot + xx
        mean = jnp.sum(tot, axis=0, keepdims=True) / ROWS
        accs = [jnp.zeros((16, 128), F32) for _ in range(11)]
        for r in range(12):
            rows = pl.ds(r * 16, 16)
            yy = xv[rows, lanes] - mean
            tt = tau[rows, lanes]
            g = gainb[rows, :]
            w = g * g
            h = g * (biasb[rows, :] - tgt[rows, lanes].astype(F32))
            wy = w * yy
            wt = w * tt
            terms = (yy * yy, wy, wy * yy, h, h * yy, tt, yy * tt, wt, wy * tt, h * tt, w)
            accs = [a + b for a, b in zip(accs, terms)]
        mom[k, 0:1, :] = mean
        for i in range(11):
            mom[k, i + 1 : i + 2, :] = jnp.sum(accs[i], axis=0, keepdims=True)
        mom[k, 12:16, :] = jnp.ones((4, 128), F32)

        @pl.when(t != 4 * k + 1)
        def _():
            send(mom.at[k], mbuf.at[t], mom_send, mom_recv, z, 4 * k + 1)

        return carry

    lax.fori_loop(0, 8, sums, 0)
    mine = lax.div(t, 4)
    is_owner = lax.rem(t, 4) == 1

    @pl.when(is_owner)
    def _():
        mbuf[t] = mom[mine]
        wait_bytes(mbuf.at[pl.ds(0, NT - 1)], mom_recv)
        s0 = mbuf[0]
        for i in range(1, NT):
            s0 = s0 + mbuf[i]
        mean = s0[0:1] / NT
        s1 = jnp.zeros((16, 128), F32)
        s2 = jnp.zeros((16, 128), F32)
        for i in range(NT):
            m = mbuf[i]
            dm = (m[0:1] - mean) * m
            s1 = s1 + dm
            s2 = s2 + (m[0:1] - mean) * dm

        def row(a, i):
            return a[i : i + 1]

        s_w = row(s0, 11)
        s_h = row(s0, 4)
        s_t = row(s0, 6)
        s_wt = row(s0, 8)
        s_ht = row(s0, 10)
        s_zz = row(s0, 1) + ROWS * row(s2, 12)
        s_wz = row(s0, 2) + row(s1, 11)
        s_wzz = row(s0, 3) + 2 * row(s1, 2) + row(s2, 11)
        s_hz = row(s0, 5) + row(s1, 4)
        s_zt = row(s0, 7) + row(s1, 6)
        s_wzt = row(s0, 9) + row(s1, 8)
        sc = 1.0 / jnp.sqrt(s_zz / D + 1e-05)
        s_wn = sc * s_wz
        s_wnn = sc * sc * s_wzz
        s_hn = sc * s_hz
        g_mean = (s_wn + s_h) / D
        g_proj = (s_wnn + s_hn) / D
        t_mean = s_t / D
        t_proj = sc * s_zt / D
        c_mean = sc * (s_wt - t_mean * s_w - t_proj * s_wn) / D
        c_proj = sc * (2 * (sc * s_wzt - t_mean * s_wn - t_proj * s_wnn) + s_ht - t_mean * s_h - t_proj * s_hn) / D
        for i, v in enumerate((mean, sc, g_mean, g_proj, t_mean, t_proj, c_mean, c_proj)):
            cbuf[mine, i : i + 1, :] = v

        def tell(i, carry):
            send(cbuf.at[mine], cbuf.at[mine], cf_send, cf_recv.at[mine], z, lax.rem(t + i, NT))
            return carry

        lax.fori_loop(1, NT, tell, 0)

    for k in range(8):

        @pl.when(t != 4 * k + 1)
        def _():
            wait_bytes(cbuf.at[k], cf_recv.at[k])

    def finish(k, carry):
        lanes = pl.ds(pl.multiple_of(k * 128, 128), 128)
        mean, sc, g_mean, g_proj, t_mean, t_proj, c_mean, c_proj = [cbuf[k, i : i + 1, :] for i in range(8)]
        lead = -sc * t_proj
        for r in range(12):
            rows = pl.ds(r * 16, 16)
            n = (xv[rows, lanes] - mean) * sc
            g = gainb[rows, :]
            w = g * g
            gn = g * (g * n + biasb[rows, :] - tgt[rows, lanes].astype(F32))
            grad = sc * (gn - g_mean - n * g_proj)
            rg[rows, lanes] = grad
            u = sc * (tau[rows, lanes] - t_mean - n * t_proj)
            cv = lead * grad + sc * (w * u - c_mean - u * g_proj - n * c_proj)
            curv[rows, :] = cv
            if r >= 8:
                curv[pl.ds(r * 16 + 64, 16), :] = cv
        curvt[pl.ds(pl.multiple_of(k * 128, 128), 128), :] = jnp.transpose(curv[...]).astype(BF16)
        return carry

    lax.fori_loop(0, 8, finish, 0)
    rg_copy = pltpu.make_async_copy(rg, rg_out, load_sem.at[5])
    rg_copy.start()

    def product(j, slot):
        rows = pl.ds(pl.multiple_of(j * 192, 64), 192)
        full = jnp.dot(ctx[rows, :], curvt[...], preferred_element_type=F32)
        lane = lax.broadcasted_iota(jnp.int32, (96, 128), 1)
        prod[slot, 0:192, :] = full[:, 0:128]
        prod[slot, 192:288, :] = jnp.where(lane < 64, full[0:96, 128:256], full[96:192, 128:256])

    def rs_sub(w, n, s):
        return rs.at[w * 9 + n, pl.ds(s * SUB, SUB), :]

    def rs_take(w, n, s):
        wait_bytes(rs_sub(w, n, s), (rsr_recv if w == 0 else rsl_recv).at[(n - 1) * 2 + s])

    def rs_pass(w, n, s):
        sem = (rsr_recv if w == 0 else rsl_recv).at[n * 2 + s]
        send(rs_sub(w, n, s), rs_sub(w, n + 1, s), rs_send, sem, z_up if w == 0 else z_down, t)

    def span(s):
        return slice(s * SUB, (s + 1) * SUB)

    product(lax.rem(z + 8, NZ), 0)
    for w in range(2):
        rs[w * 9, span(w), :] = prod[0, span(w), :]
        rs_pass(w, 0, w)
    for n in range(1, 8):
        product(lax.rem(z + 8 - n, NZ), 0)
        product(lax.rem(z + 8 + n, NZ), 1)
        for first in (True, False):
            for w in range(2):
                s = 1 - w if first else w
                if n == 1 and first:
                    rs[w * 9 + n, span(s), :] = prod[w, span(s), :]
                else:
                    rs_take(w, n, s)
                    rs[w * 9 + n, span(s), :] = rs[w * 9 + n, span(s), :] + prod[w, span(s), :]
                rs_pass(w, n, s)
    product(z, 0)
    pair = stk[192:384, pl.ds(pl.multiple_of(lax.div(z, 2) * 384, 128), 384)].astype(F32)
    pc = jnp.where(lax.rem(z, 2) == 0, pair[:, 0:192], pair[:, 192:384]) * (1.0 / TOKENS)
    for w in range(2):
        for s in range(2):
            rs_take(w, 8, s)
    both = prod[0] + rs[8] + rs[17]
    at = jnp.transpose(both[0:192])
    bt = jnp.transpose(both[192:288])
    hess_ref[0:128, :] = pc[0:128] * at
    hess_ref[128:192, 0:96] = pc[128:192, 0:96] * bt[0:64]
    hess_ref[128:192, 96:192] = pc[128:192, 96:192] * bt[64:128]

    rg_copy.wait()
    wait_bytes(ctx.at[pl.ds(0, 31 * BLK), :], ctx_send)
    wait_bytes(pk.at[pl.ds(0, 15)], pk_send)
    wait_bytes(rs.at[pl.ds(0, 15)], rs_send)

    @pl.when(is_owner)
    def _():
        wait_bytes(mom.at[pl.ds(0, 7)], mom_send)
        wait_bytes(rs.at[0, pl.ds(0, 8 * (NT - 1)), :], cf_send)

    @pl.when(jnp.logical_not(is_owner))
    def _():
        wait_bytes(mom, mom_send)


def shards(context, residual, out_weight, norm_gain, norm_bias, target, probe):
    hbm = pl.BlockSpec(memory_space=pltpu.HBM)
    anywhere = pl.BlockSpec(memory_space=pl.ANY)
    vmem = pl.BlockSpec(memory_space=pltpu.VMEM)
    dma = pltpu.SemaphoreType.DMA
    arrays = (context, residual, out_weight, norm_gain.reshape(1, ROWS), norm_bias.reshape(1, ROWS), target, probe)
    arrays = [pltpu.with_memory_space_constraint(a, pltpu.HBM) for a in arrays]
    return pl.pallas_call(
        kernel,
        out_shape=(
            jax.ShapeDtypeStruct((ROWS, 192), F32),
            jax.ShapeDtypeStruct((ROWS, TOK), F32),
        ),
        in_specs=[hbm] * 7,
        out_specs=(vmem, anywhere),
        scratch_shapes=[
            pltpu.VMEM((NT * BLK, TOK), BF16),
            pltpu.VMEM((2 * ROWS, 3072), BF16),
            pltpu.VMEM((NZ, PK, 128), BF16),
            pltpu.VMEM((192, 192), BF16),
            pltpu.VMEM((ROWS, TOK), BF16),
            pltpu.VMEM((ROWS, TOK), BF16),
            pltpu.VMEM((ROWS, TOK), F32),
            pltpu.VMEM((ROWS, TOK), F32),
            pltpu.VMEM((1, ROWS), F32),
            pltpu.VMEM((1, ROWS), F32),
            pltpu.VMEM((ROWS, 128), F32),
            pltpu.VMEM((ROWS, 128), F32),
            pltpu.VMEM((8, 16, 128), F32),
            pltpu.VMEM((NT, 16, 128), F32),
            pltpu.VMEM((8, 8, 128), F32),
            pltpu.VMEM((256, 128), F32),
            pltpu.VMEM((TOK, 256), BF16),
            pltpu.VMEM((ROWS, TOK), F32),
            pltpu.VMEM((18, PK, 128), F32),
            pltpu.VMEM((2, PK, 128), F32),
            dma((8,)),
            dma,
            dma((4,)),
            dma((24,)),
            dma((16,)),
            dma,
            dma((16,)),
            dma((16,)),
            dma,
            dma,
            dma,
            dma((8,)),
            dma,
            dma((16,)),
            dma((16,)),
        ],
        compiler_params=pltpu.CompilerParams(
            collective_id=0, has_side_effects=True, vmem_limit_bytes=48 * 1024 * 1024
        ),
    )(*arrays)


def solution(mesh):
    return jax.shard_map(
        shards,
        mesh=mesh,
        in_specs=(
            P("tensor", "dp"),
            P("tensor", "dp"),
            P("tensor", "dp"),
            P("tensor"),
            P("tensor"),
            P("tensor", "dp"),
            P("tensor", None),
        ),
        out_specs=(P("tensor", "dp"), P("tensor", "dp")),
        check_vma=False,
    )
```

time: 120 us -> 92 us (0.77)
  the two profiles are of different devices: /device:TPU:4 before, /device:TPU:32 now
where the time goes in v2:
time: 92 us; the launch traced here: 91.9 us
  Pallas kernels  89.7 us (98%)
  local copies, waits for them, and re-layouts  1.56 us (2%)
    pallas_call x1, Pallas kernels, shards(): pl.pallas_call(kernel, out_shape=(jax.ShapeDtypeStruct((ROWS, 192), F32),...  89.7 us

profile of v2, /device:TPU:32, one launch (start us, length us, event | category | flops | bytes accessed | tf_op | source)
XLA Modules:
  0.0 91.9 jit_solution(654880184439922969)
XLA Ops:
  0.6 89.7 %shard_map.86 = (f32[192,192]{1,0:T(8,128)S(1)}, f32[192,1024]{1,0:T(8,128)S(1)}) custom-call(bf16[96,1024]{1,0:T(8,128)(2,1)} %ctx_in.1, bf16[192,1024]{1,0:T(8,128)(2,1)} %res_in.1, bf16[192,192]{1,0:T(8,128)(2,1)} %w_in.1, f32[1,192]{1,0:T(1,128)} %bitcast.2, f32[1,192]{1,0:T(1,128)} %bitcast.3, bf16[192,1024]{1,0:T(8,128)(2,1)} %tgt_in.1, ...), custom_call_target="tpu_custom_call" | custom-call | tf_op jit(solution)/shard_map/pallas_call | solution.py:384
  90.3 0.7 copy.11
  91.0 0.9 copy.12

commit v3 on v2

v3 whole, which is shorter than its diff:
```python
import jax
import jax.numpy as jnp
from jax import lax
from jax.experimental import pallas as pl
from jax.experimental.pallas import tpu as pltpu
from jax.sharding import PartitionSpec as P

MESH = pl.DeviceIdType.MESH
F32 = jnp.float32
BF16 = jnp.bfloat16

D = 6144
ROWS = 192
TOK = 1024
BLK = 96
NZ = 16
NT = 32
PK = 288
ZSUB = 192
RSUB = 144
RMSG = 224
LOW = 2.0**-8 / 10
FAST = 2 * 3
TOKENS = 16384

PLAN = (
    (
        ("S", "p", 1), ("S", "p", -1), ("S", "q", 0, 1), ("S", "q", 0, -1), ("W", "p", 1), ("S", "q", 1, 1),
        ("W", "p", -1), ("S", "q", -1, -1), ("W", "q", 0, 1), ("S", "p2", 0), ("S", "p2", 1), ("S", "qq", 0, 1),
        ("W", "p2", 0), ("S", "q2h", 0, -1), ("S", "q", -1, 1), ("W", "p2", 1), ("W", "q", -1, -1),
        ("S", "q2h", 1, 1), ("S", "q", 1, -1), ("W", "q", 0, -1), ("W", "q", 1, 1), ("S", "qq", -1, 0),
        ("S", "q2h", 0, 1), ("S", "qq", 1, 1), ("S", "qq", 0, 0), ("W", "q2h", 0, -1), ("S", "q2h", 1, -1),
        ("W", "q2h", 1, 1), ("S", "qq", 2, 1), ("S", "qq", 2, 0), ("W", "q", -1, 1), ("W", "q", 1, -1),
        ("S", "qq", 1, 0), ("S", "qq", -1, 1), ("W", "q2h", 0, 1), ("W", "qq", 2, 1), ("W", "qq", -1, 0),
        ("W", "qq", 2, 0), ("W", "q2h", 1, -1), ("W", "qq", -1, 1), ("W", "qq", 0, 1), ("W", "qq", 1, 1),
        ("W", "qq", 0, 0), ("W", "qq", 1, 0),
    ),
    (
        ("S", "p", -1), ("S", "zd", 2, 0), ("S", "zu", 2, 0), ("S", "p", 1), ("S", "q", 0, -1), ("S", "zu", 2, 1),
        ("S", "zd", 1, 0), ("S", "zu", 2, 2), ("S", "zd", 2, 2), ("S", "zd", 2, 1), ("W", "p", -1), ("S", "zd", 1, 2),
        ("S", "zu", 1, 0), ("W", "p", 1), ("S", "q", 1, 1), ("S", "q", -1, -1), ("S", "q", 1, -1), ("S", "q", -1, 1),
        ("S", "p2", 1), ("S", "zd", 1, 1), ("S", "zu", 1, 1), ("W", "zu", 2, 0), ("S", "zu", 4, 0), ("S", "p2", 0),
        ("W", "zd", 2, 0), ("S", "zd", 4, 0), ("W", "zu", 2, 2), ("W", "zu", 2, 1), ("W", "zd", 2, 2),
        ("S", "zu", 3, 1), ("W", "zd", 2, 1), ("S", "zu", 1, 2), ("S", "zd", 4, 2), ("W", "q", 0, -1),
        ("S", "zu", 4, 1), ("S", "zd", 3, 0), ("W", "zd", 1, 1), ("W", "p2", 0), ("S", "zd", 4, 1), ("S", "zu", 4, 2),
        ("S", "q", 0, 1), ("W", "zu", 4, 0), ("S", "zd", 3, 2), ("S", "q2h", 0, -1), ("W", "zd", 4, 0),
        ("S", "zu", 6, 0), ("S", "zd", 5, 0), ("W", "zd", 4, 2), ("S", "zd", 6, 2), ("S", "zu", 5, 0),
        ("W", "zu", 4, 1), ("S", "zu", 6, 1), ("W", "zd", 3, 0), ("W", "q", -1, -1), ("W", "zu", 1, 1),
        ("W", "q", -1, 1), ("S", "qq", -1, 1), ("W", "p2", 1), ("W", "zd", 1, 0), ("W", "q", 1, -1),
        ("S", "q2h", 1, 1), ("W", "zu", 1, 0), ("W", "q", 1, 1), ("S", "qq", 0, 0), ("S", "zd", 6, 0),
        ("W", "zu", 1, 2), ("W", "zu", 4, 2), ("S", "zu", 6, 2), ("W", "zd", 4, 1), ("S", "zd", 6, 1),
        ("W", "zu", 6, 0), ("S", "zu", 3, 0), ("W", "q2h", 0, -1), ("S", "qq", -1, 0), ("W", "zd", 3, 2),
        ("S", "qq", 2, 0), ("S", "q2h", 0, 1), ("S", "qq", 1, 0), ("W", "zd", 5, 0), ("S", "zd", 5, 2),
        ("W", "zu", 5, 0), ("S", "zu", 5, 1), ("S", "zu", 7, 0), ("W", "zd", 6, 2), ("S", "zd", 7, 2),
        ("W", "zu", 3, 1), ("S", "qq", 1, 1), ("W", "q", 0, 1), ("S", "qq", 0, 1), ("W", "zu", 6, 1),
        ("S", "zu", 7, 1), ("S", "zd", 5, 1), ("W", "q2h", 1, 1), ("S", "zu", 5, 2), ("S", "zd", 3, 1),
        ("S", "qq", 2, 1), ("W", "zu", 6, 2), ("S", "zu", 3, 2), ("W", "zd", 6, 0), ("S", "zu", 7, 2),
        ("S", "zd", 7, 0), ("W", "zd", 6, 1), ("S", "zd", 7, 1), ("S", "q2h", 1, -1), ("W", "zu", 5, 1),
        ("W", "zu", 7, 0), ("S", "zu", 8, 0), ("W", "zd", 7, 2), ("S", "zd", 8, 2), ("W", "zu", 3, 0),
        ("W", "zu", 7, 1), ("S", "zu", 8, 1), ("W", "qq", 0, 0), ("W", "zu", 5, 2), ("W", "qq", 2, 0),
        ("W", "zu", 7, 2), ("W", "qq", 1, 0), ("W", "zd", 5, 2), ("W", "zd", 3, 1), ("W", "qq", -1, 0),
        ("W", "zd", 7, 1), ("W", "q2h", 0, 1), ("W", "zd", 5, 1), ("W", "zu", 3, 2), ("W", "qq", 2, 1),
        ("W", "q2h", 1, -1), ("W", "zd", 1, 2), ("W", "zu", 8, 0), ("W", "qq", 0, 1), ("W", "zd", 7, 0),
        ("W", "qq", -1, 1), ("W", "qq", 1, 1), ("W", "zd", 8, 2), ("W", "zu", 8, 1),
    ),
)

def kernel(
    ctx_in, res_in, w_in, gain_in, bias_in, tgt_in, probe_in,
    hess_ref, rg_out,
    ctx, stk, pk, wloc, res, tgt, xv, tau, grow, brow, gainb, biasb, mom, mbuf, cbuf, curv, curvt, rg, rs, prod, prod0, back,
    load_sem, ctx_send, p_recv, q_recv, c_recv, pk_send, pkr_recv, pkl_recv, w_send, w_recv,
    mom_send, mom_recv, cf_send, cf_recv, rs_send, rsr_recv, rsl_recv, prod_send, prod_recv, back_send, back_recv,
):
    z = lax.axis_index("dp")
    t = lax.axis_index("tensor")
    core = lax.rem(t, 2)
    x = lax.div(t, 8)
    y = lax.rem(lax.div(t, 2), 4)
    other = t + 1 - 2 * core
    is_one = core == 1
    is_zero = core == 0

    def plane(n):
        return lax.rem(z + n + NZ, NZ)


    def wait_bytes(ref, sem):
        pltpu.make_async_copy(ref, ref, sem).wait()

    def send(src, dst, ssem, rsem, zz, tt):
        pltpu.make_async_remote_copy(
            src_ref=src, dst_ref=dst, send_sem=ssem, recv_sem=rsem, device_id=(zz, tt), device_id_type=MESH
        ).start()

    barrier = pltpu.get_barrier_semaphore()
    for n in (1, -1, 2, -2):
        pl.semaphore_signal(barrier, inc=1, device_id=(plane(n), t), device_id_type=MESH)

    def greet(i, carry):
        pl.semaphore_signal(barrier, inc=1, device_id=(z, lax.rem(t + i, NT)), device_id_type=MESH)
        return carry

    lax.fori_loop(1, NT, greet, 0)

    own_rows = pl.ds(pl.multiple_of(t * BLK, 32), BLK)
    own = ctx.at[own_rows, :]
    loads = [
        pltpu.make_async_copy(w_in, wloc, load_sem.at[0]),
        pltpu.make_async_copy(probe_in, stk.at[pl.ds(ROWS, ROWS), :], load_sem.at[1]),
        pltpu.make_async_copy(ctx_in, own, load_sem.at[2]),
        pltpu.make_async_copy(res_in, res, load_sem.at[3]),
        pltpu.make_async_copy(tgt_in, tgt, load_sem.at[4]),
        pltpu.make_async_copy(gain_in, grow, load_sem.at[6]),
        pltpu.make_async_copy(bias_in, brow, load_sem.at[7]),
    ]
    for c in loads:
        c.start()
    loads[0].wait()
    half_at = pl.multiple_of((1 - core) * PK, 32)
    pk[z, pl.ds(half_at, 192), :] = wloc[:, 0:128]
    pk[z, pl.ds(half_at + 192, 96), 0:64] = wloc[0:96, 128:192]
    pk[z, pl.ds(half_at + 192, 96), 64:128] = wloc[96:192, 128:192]
    pl.semaphore_wait(barrier, NT + 3)

    def zero_half(j):
        return pk.at[j, pl.ds(PK, PK), :]

    def pk_sub(j, s):
        return pk.at[j, pl.ds(s * ZSUB, ZSUB), :]

    def gather(c):
        p, q = (y, x) if c else (x, y)
        sp, sq = (2, 8) if c else (8, 2)

        def dev(dp, dq):
            return lax.rem(p + dp + 4, 4) * sp + lax.rem(q + dq + 4, 4) * sq + c

        def blk(dp, dq, half=None):
            rows = pl.ds(pl.multiple_of(dev(dp, dq) * BLK, 32), BLK)
            if half is None:
                return ctx.at[rows, :]
            return ctx.at[rows, pl.ds(half * 512, 512)]

        def to_core(dp, dq, src=None):
            b = blk(dp, dq)
            send(b if src is None else src, b, ctx_send, c_recv.at[(dp % 4) * 4 + dq % 4], z, other)

        def route(kind, a, b=None):
            if kind == "p":
                return blk(a, 0), p_recv.at[0 if a < 0 else 1], (0, 0, None), (-a, 0)
            if kind == "p2":
                d = -1 if a == 0 else 1
                return blk(2, 0, a), p_recv.at[2 + a], (d, 0, a), (-d, 0)
            if kind == "q":
                return blk(a, b), q_recv.at[(a % 4) * 6 + (0 if b < 0 else 1)], (a, 0, None), (0, -b)
            if kind == "q2h":
                return blk(2, b, a), q_recv.at[12 + (0 if b < 0 else 1) + 2 * a], (2, 0, a), (0, -b)
            d = -1 if b == 0 else 1
            return blk(a, 2, b), q_recv.at[(a % 4) * 6 + 4 + b], (a, d, b), (0, -d)

        if c == 0:
            send(zero_half(z), zero_half(z), w_send, w_recv.at[0], z, other)
        arrived = set()
        for act, kind, *ab in PLAN[c]:
            if kind in ("zu", "zd"):
                n, s = ab
                sign = 1 if kind == "zu" else -1
                sem = (pkr_recv if kind == "zu" else pkl_recv).at[(n - 1) * 3 + s]
                hop = 2 if n <= FAST and n % 2 == 0 else 1
                if act == "S":
                    if n == hop and "w" not in arrived:
                        arrived.add("w")
                        wait_bytes(zero_half(z), w_recv.at[0])
                    ref = pk_sub(plane(sign * (hop - n)), s)
                    send(ref, ref, pk_send, sem, plane(sign * hop), t)
                else:
                    j = plane(-sign * n)
                    wait_bytes(pk_sub(j, s), sem)
                    key = n if n == 8 else (kind, n)
                    arrived.add((key, s))
                    if s > 0 and (key, 3 - s) in arrived:
                        send(zero_half(j), zero_half(j), w_send, w_recv.at[n if kind == "zu" or n == 8 else 16 - n], z, other)
                continue
            dst, sem, (dp, dq, half), to = route(kind, *ab)
            if act == "S":
                src = blk(dp, dq, half)
                if (dp, dq) == (0, 0):
                    send(ctx_in, src, ctx_send, sem, z, dev(*to))
                    if kind == "q" and ab[1] == 1:
                        to_core(0, 0, ctx_in)
                else:
                    send(src, src, ctx_send, sem, z, dev(*to))
                continue
            wait_bytes(dst, sem)
            arrived.add((kind, *ab))
            if kind == "p":
                to_core(ab[0], 0)
            elif kind == "q":
                to_core(*ab)
            elif kind == "p2" and ("p2", 1 - ab[0]) in arrived:
                to_core(2, 0)
            elif kind == "q2h" and ("q2h", 1 - ab[0], ab[1]) in arrived:
                to_core(2, ab[1])
            elif kind == "qq" and ("qq", ab[0], 1 - ab[1]) in arrived:
                to_core(ab[0], 2)
        if c == 0:
            for n in range(1, NZ):
                wait_bytes(zero_half(plane(-n)), w_recv.at[n])
        for dp in range(4):
            for dq in range(4):
                o = lax.rem(q + dp + 4, 4) * sq + lax.rem(p + dq + 4, 4) * sp + 1 - c
                rows = pl.ds(pl.multiple_of(o * BLK, 32), BLK)
                wait_bytes(ctx.at[rows, :], c_recv.at[dp * 4 + dq])

    @pl.when(is_zero)
    def _():
        gather(0)

    @pl.when(is_one)
    def _():
        gather(1)

    for c in loads[5:]:
        c.wait()
    gainb[...] = jnp.transpose(jnp.broadcast_to(grow[...], (128, ROWS)))
    biasb[...] = jnp.transpose(jnp.broadcast_to(brow[...], (128, ROWS)))
    for j in range(NZ):
        c = 192 * j
        stk[0:192, c : c + 128] = pk[j, pl.ds(half_at, 192), :]
        stk[0:96, c + 128 : c + 192] = pk[j, pl.ds(half_at + 192, 96), 0:64]
        stk[96:192, c + 128 : c + 192] = pk[j, pl.ds(half_at + 192, 96), 64:128]

    for c in loads[1:5]:
        c.wait()

    for n in range(2):
        cols = slice(n * 512, (n + 1) * 512)
        both = jnp.dot(stk[...], ctx[:, cols], preferred_element_type=F32)
        xv[:, cols] = both[0:192]
        tau[:, cols] = both[192:384]

    def sums(k, carry):
        lanes = pl.ds(pl.multiple_of(k * 128, 128), 128)
        tot = jnp.zeros((16, 128), F32)
        for r in range(12):
            rows = pl.ds(r * 16, 16)
            xx = xv[rows, lanes] + res[rows, lanes].astype(F32)
            xv[rows, lanes] = xx
            tot = tot + xx
        mean = jnp.sum(tot, axis=0, keepdims=True) / ROWS
        accs = [jnp.zeros((16, 128), F32) for _ in range(11)]
        for r in range(12):
            rows = pl.ds(r * 16, 16)
            yy = xv[rows, lanes] - mean
            tt = tau[rows, lanes]
            g = gainb[rows, :]
            w = g * g
            h = g * (biasb[rows, :] - tgt[rows, lanes].astype(F32))
            wy = w * yy
            wt = w * tt
            terms = (yy * yy, wy, wy * yy, h, h * yy, tt, yy * tt, wt, wy * tt, h * tt, w)
            accs = [a + b for a, b in zip(accs, terms)]
        mom[k, 0:1, :] = mean
        for i in range(11):
            mom[k, i + 1 : i + 2, :] = jnp.sum(accs[i], axis=0, keepdims=True)
        mom[k, 12:16, :] = jnp.ones((4, 128), F32)

        @pl.when(t != 4 * k + 1)
        def _():
            send(mom.at[k], mbuf.at[t], mom_send, mom_recv, z, 4 * k + 1)

        return carry

    lax.fori_loop(0, 8, sums, 0)
    mine = lax.div(t, 4)
    is_owner = lax.rem(t, 4) == 1

    @pl.when(is_owner)
    def _():
        mbuf[t] = mom[mine]
        wait_bytes(mbuf.at[pl.ds(0, NT - 1)], mom_recv)
        s0 = mbuf[0]
        for i in range(1, NT):
            s0 = s0 + mbuf[i]
        mean = s0[0:1] / NT
        s1 = jnp.zeros((16, 128), F32)
        s2 = jnp.zeros((16, 128), F32)
        for i in range(NT):
            m = mbuf[i]
            dm = (m[0:1] - mean) * m
            s1 = s1 + dm
            s2 = s2 + (m[0:1] - mean) * dm

        def row(a, i):
            return a[i : i + 1]

        s_w = row(s0, 11)
        s_h = row(s0, 4)
        s_t = row(s0, 6)
        s_wt = row(s0, 8)
        s_ht = row(s0, 10)
        s_zz = row(s0, 1) + ROWS * row(s2, 12)
        s_wz = row(s0, 2) + row(s1, 11)
        s_wzz = row(s0, 3) + 2 * row(s1, 2) + row(s2, 11)
        s_hz = row(s0, 5) + row(s1, 4)
        s_zt = row(s0, 7) + row(s1, 6)
        s_wzt = row(s0, 9) + row(s1, 8)
        sc = 1.0 / jnp.sqrt(s_zz / D + 1e-05)
        s_wn = sc * s_wz
        s_wnn = sc * sc * s_wzz
        s_hn = sc * s_hz
        g_mean = (s_wn + s_h) / D
        g_proj = (s_wnn + s_hn) / D
        t_mean = s_t / D
        t_proj = sc * s_zt / D
        c_mean = sc * (s_wt - t_mean * s_w - t_proj * s_wn) / D
        c_proj = sc * (2 * (sc * s_wzt - t_mean * s_wn - t_proj * s_wnn) + s_ht - t_mean * s_h - t_proj * s_hn) / D
        for i, v in enumerate((mean, sc, g_mean, g_proj, t_mean, t_proj, c_mean, c_proj)):
            cbuf[mine, i : i + 1, :] = v

        def tell(i, carry):
            send(cbuf.at[mine], cbuf.at[mine], cf_send, cf_recv.at[mine], z, lax.rem(t + i, NT))
            return carry

        lax.fori_loop(1, NT, tell, 0)

    for k in range(8):

        @pl.when(t != 4 * k + 1)
        def _():
            wait_bytes(cbuf.at[k], cf_recv.at[k])

    def finish(k, carry):
        lanes = pl.ds(pl.multiple_of(k * 128, 128), 128)
        mean, sc, g_mean, g_proj, t_mean, t_proj, c_mean, c_proj = [cbuf[k, i : i + 1, :] for i in range(8)]
        lead = -sc * t_proj
        for r in range(12):
            rows = pl.ds(r * 16, 16)
            n = (xv[rows, lanes] - mean) * sc
            g = gainb[rows, :]
            w = g * g
            gn = g * (g * n + biasb[rows, :] - tgt[rows, lanes].astype(F32))
            grad = sc * (gn - g_mean - n * g_proj)
            rg[rows, lanes] = grad
            u = sc * (tau[rows, lanes] - t_mean - n * t_proj)
            cv = lead * grad + sc * (w * u - c_mean - u * g_proj - n * c_proj)
            curv[rows, :] = cv
            if r >= 8:
                curv[pl.ds(r * 16 + 64, 16), :] = cv
        curvt[pl.ds(pl.multiple_of(k * 128, 128), 128), :] = jnp.transpose(curv[...]).astype(BF16)
        return carry

    lax.fori_loop(0, 8, finish, 0)
    rg_copy = pltpu.make_async_copy(rg, rg_out, load_sem.at[5])
    rg_copy.start()

    def product(j, slot):
        rows = pl.ds(pl.multiple_of(j * 192, 64), 192)
        full = jnp.dot(ctx[rows, :], curvt[...], preferred_element_type=F32)
        lane = lax.broadcasted_iota(jnp.int32, (96, 128), 1)
        prod[slot, 0:192, :] = full[:, 0:128]
        prod[slot, 192:288, :] = jnp.where(lane < 64, full[0:96, 128:256], full[96:192, 128:256])

    def wanted(i):
        return plane(8 + (1 - 2 * lax.rem(i, 2)) * lax.div(i + 1, 2))

    def finish_hess(both):
        pair = stk[192:384, pl.ds(pl.multiple_of(lax.div(z, 2) * 384, 128), 384)].astype(F32)
        pc = jnp.where(lax.rem(z, 2) == 0, pair[:, 0:192], pair[:, 192:384]) * (1.0 / TOKENS)
        at = jnp.transpose(both[0:192])
        bt = jnp.transpose(both[192:288])
        hess_ref[0:128, :] = pc[0:128] * at
        hess_ref[128:192, 0:96] = pc[128:192, 0:96] * bt[0:64]
        hess_ref[128:192, 96:192] = pc[128:192, 96:192] * bt[64:128]

    @pl.when(is_zero)
    def _():
        def hand(i, carry):
            product(wanted(i), i)
            send(prod.at[i], prod0.at[i], prod_send, prod_recv.at[i], z, other)
            return carry

        lax.fori_loop(0, NZ - 1, hand, 0)
        product(z, NZ - 1)
        wait_bytes(back.at[0], back_recv)
        finish_hess(back[0] + prod[NZ - 1])
        wait_bytes(prod.at[pl.ds(0, NZ - 1)], prod_send)

    @pl.when(is_one)
    def _():
        def rs_sub(w, n, s):
            return rs.at[(w * 9 + n) * 4 + s]

        def rs_take(w, n, s):
            wait_bytes(rs_sub(w, n, s), (rsr_recv if w == 0 else rsl_recv).at[(n - 1) * 4 + s])

        def rs_pass(w, n, s):
            sem = (rsr_recv if w == 0 else rsl_recv).at[n * 4 + s]
            send(rs_sub(w, n, s), rs_sub(w, n + 1, s), rs_send, sem, plane(1 - 2 * w), t)

        def own(i, s):
            lo = s % 2 * RSUB
            return (prod if s < 2 else prod0)[i, lo : lo + RSUB, :]

        def code(w, n, s, v):
            at = (w * 9 + n) * 4 + s
            high = v.astype(BF16)
            near = high.astype(F32)
            rest = jnp.where(jnp.abs(near) > 1e-30, (v - near) * pl.reciprocal(near, approx=True), 0.0)
            steps = jnp.round(rest * (1 / LOW))
            rs[at, 0:RSUB, :] = high
            rs[at, RSUB : RSUB + 64, :] = (21 * steps[0:64] + steps[80:RSUB]).astype(BF16)
            rs[at, RSUB + 64 : RMSG, :] = (21 * steps[64:80]).astype(BF16)

        def decode(w, n, s):
            at = (w * 9 + n) * 4 + s
            near = rs[at, 0:RSUB, :].astype(F32)
            low = rs[at, RSUB:RMSG, :].astype(F32)
            one = jnp.round(low * (1 / 21))
            two = low - 21 * one
            steps = jnp.concatenate([one, two[0:64]], axis=0)
            return near + near * (steps * LOW)

        def put(w, n, i, s, add):
            v = own(i, s)
            if add:
                rs_take(w, n, s)
                v = v + decode(w, n, s)
            code(w, n, s, v)
            rs_pass(w, n, s)

        def theirs(i):
            wait_bytes(prod0.at[i], prod_recv.at[i])

        product(wanted(0), 0)
        for s in (0, 1):
            put(0, 0, 0, s, False)
        theirs(0)
        for s in (2, 3):
            put(1, 0, 0, s, False)
        for n in range(1, 8):
            for w in range(2):
                product(wanted(2 * n - 1 + w), 2 * n - 1 + w)
            if n == 1:
                for s in (0, 1):
                    put(1, 1, 2, s, False)
                theirs(1)
                for s in (2, 3):
                    put(0, 1, 1, s, False)
                theirs(2)
                for s in (0, 1):
                    put(0, 1, 1, s, True)
                    put(1, 1, 2, s + 2, True)
                continue
            theirs(2 * n - 1)
            theirs(2 * n)
            for s in (2, 3, 0, 1):
                put(0, n, 2 * n - 1, s, True)
                put(1, n, 2 * n, s ^ 2, True)
        product(z, NZ - 1)
        for s in (2, 3):
            for w in range(2):
                rs_take(w, 8, s)
        back[1, 0:RSUB, :] = decode(0, 8, 2) + decode(1, 8, 2)
        back[1, RSUB:PK, :] = decode(0, 8, 3) + decode(1, 8, 3)
        send(back.at[1], back.at[0], back_send, back_recv, z, other)
        for s in (0, 1):
            for w in range(2):
                rs_take(w, 8, s)
        finish_hess(prod[NZ - 1] + jnp.concatenate([decode(0, 8, s) + decode(1, 8, s) for s in (0, 1)], axis=0))
        wait_bytes(back.at[0], back_send)
        wait_bytes(rs.at[pl.ds(0, 60)], rs_send)
        wait_bytes(pk.at[pl.ds(0, 15)], pk_send)
        wait_bytes(pk.at[pl.ds(0, 15), pl.ds(0, PK), :], w_send)

    rg_copy.wait()
    wait_bytes(ctx.at[pl.ds(0, 31 * BLK), :], ctx_send)

    @pl.when(is_zero)
    def _():
        wait_bytes(pk.at[0, pl.ds(0, PK), :], w_send)

    @pl.when(is_owner)
    def _():
        wait_bytes(mom.at[pl.ds(0, 7)], mom_send)
        wait_bytes(prod.at[0, pl.ds(0, 8 * (NT - 1)), :], cf_send)

    @pl.when(jnp.logical_not(is_owner))
    def _():
        wait_bytes(mom, mom_send)


def shards(context, residual, out_weight, norm_gain, norm_bias, target, probe):
    hbm = pl.BlockSpec(memory_space=pltpu.HBM)
    anywhere = pl.BlockSpec(memory_space=pl.ANY)
    vmem = pl.BlockSpec(memory_space=pltpu.VMEM)
    dma = pltpu.SemaphoreType.DMA
    arrays = (context, residual, out_weight, norm_gain.reshape(1, ROWS), norm_bias.reshape(1, ROWS), target, probe)
    arrays = [pltpu.with_memory_space_constraint(a, pltpu.HBM) for a in arrays]
    return pl.pallas_call(
        kernel,
        out_shape=(
            jax.ShapeDtypeStruct((ROWS, 192), F32),
            jax.ShapeDtypeStruct((ROWS, TOK), F32),
        ),
        in_specs=[hbm] * 7,
        out_specs=(vmem, anywhere),
        scratch_shapes=[
            pltpu.VMEM((NT * BLK, TOK), BF16),
            pltpu.VMEM((2 * ROWS, 3072), BF16),
            pltpu.VMEM((NZ, 2 * PK, 128), BF16),
            pltpu.VMEM((192, 192), BF16),
            pltpu.VMEM((ROWS, TOK), BF16),
            pltpu.VMEM((ROWS, TOK), BF16),
            pltpu.VMEM((ROWS, TOK), F32),
            pltpu.VMEM((ROWS, TOK), F32),
            pltpu.VMEM((1, ROWS), F32),
            pltpu.VMEM((1, ROWS), F32),
            pltpu.VMEM((ROWS, 128), F32),
            pltpu.VMEM((ROWS, 128), F32),
            pltpu.VMEM((8, 16, 128), F32),
            pltpu.VMEM((NT, 16, 128), F32),
            pltpu.VMEM((8, 8, 128), F32),
            pltpu.VMEM((256, 128), F32),
            pltpu.VMEM((TOK, 256), BF16),
            pltpu.VMEM((ROWS, TOK), F32),
            pltpu.VMEM((18 * 4, RMSG, 128), BF16),
            pltpu.VMEM((NZ, PK, 128), F32),
            pltpu.VMEM((NZ, PK, 128), F32),
            pltpu.VMEM((2, PK, 128), F32),
            dma((8,)),
            dma,
            dma((4,)),
            dma((24,)),
            dma((16,)),
            dma,
            dma((24,)),
            dma((24,)),
            dma,
            dma((16,)),
            dma,
            dma,
            dma,
            dma((8,)),
            dma,
            dma((32,)),
            dma((32,)),
            dma,
            dma((16,)),
            dma,
            dma,
        ],
        compiler_params=pltpu.CompilerParams(
            collective_id=0, has_side_effects=True, vmem_limit_bytes=48 * 1024 * 1024
        ),
    )(*arrays)


def solution(mesh):
    return jax.shard_map(
        shards,
        mesh=mesh,
        in_specs=(
            P("tensor", "dp"),
            P("tensor", "dp"),
            P("tensor", "dp"),
            P("tensor"),
            P("tensor"),
            P("tensor", "dp"),
            P("tensor", None),
        ),
        out_specs=(P("tensor", "dp"), P("tensor", "dp")),
        check_vma=False,
    )
```

time: 92 us -> 84.4 us (0.917)
  the two profiles are of different devices: /device:TPU:32 before, /device:TPU:1 now
where the time goes in v3:
time: 84.4 us; the launch traced here: 84.2 us
  Pallas kernels  82 us (97%)
  local copies, waits for them, and re-layouts  1.56 us (2%)
    pallas_call x1, Pallas kernels, shards(): pl.pallas_call(kernel, out_shape=(jax.ShapeDtypeStruct((ROWS, 192), F32),...  82 us

profile of v3, /device:TPU:1, one launch (start us, length us, event | category | flops | bytes accessed | tf_op | source)
XLA Modules:
  0.0 84.2 jit_solution(3882898166624600859)
XLA Ops:
  0.6 82.0 %shard_map.86 = (f32[192,192]{1,0:T(8,128)S(1)}, f32[192,1024]{1,0:T(8,128)S(1)}) custom-call(bf16[96,1024]{1,0:T(8,128)(2,1)} %ctx_in.1, bf16[192,1024]{1,0:T(8,128)(2,1)} %res_in.1, bf16[192,192]{1,0:T(8,128)(2,1)} %w_in.1, f32[1,192]{1,0:T(1,128)} %bitcast.2, f32[1,192]{1,0:T(1,128)} %bitcast.3, bf16[192,1024]{1,0:T(8,128)(2,1)} %tgt_in.1, ...), custom_call_target="tpu_custom_call" | custom-call | tf_op jit(solution)/shard_map/pallas_call | solution.py:501
  82.7 0.7 copy.11
  83.4 0.9 %copy.12 = f32[192,1024]{1,0:T(8,128)} copy(f32[192,1024]{1,0:T(8,128)S(1)} %get-tuple-element.5) | data formatting | bytes 1572864

commit v4 on v3

v4 whole, which is shorter than its diff:
```python
import jax
import jax.numpy as jnp
from jax import lax
from jax.experimental import pallas as pl
from jax.experimental.pallas import tpu as pltpu
from jax.sharding import PartitionSpec as P

MESH = pl.DeviceIdType.MESH
F32 = jnp.float32
BF16 = jnp.bfloat16

D = 6144
ROWS = 192
TOK = 1024
BLK = 96
NZ = 16
NT = 32
PK = 288
ZSUB = 192
RSUB = 144
RMSG = 224
LOW = 2.0**-8 / 10
GROUPS = ((0, 1), (1, 2), (2, 3), (3, 5), (5, 7), (7, 15))
FAST = 2 * 3
TOKENS = 16384

PLAN = (
    (
        ("S", "Q0"), ("S", "P"), ("W", "P"), ("W", "Q0"), ("S", "QQ0"), ("S", "cP"), ("S", "Q1"), ("S", "P2"),
        ("W", "QQ0"), ("W", "P2"), ("S", "cQ0"), ("S", "QA"), ("S", "QB"), ("W", "Q1"), ("S", "QQ1"), ("W", "QA"),
        ("S", "cP2"), ("S", "QQ2"), ("S", "cQQ0"), ("W", "QB"), ("S", "cQ1"), ("S", "cQ2"), ("W", "QQ1"),
        ("S", "cQQ1"), ("W", "QQ2"), ("S", "cQQ2"), ("S", "cO"),
    ),
    (
        ("S", "z", 1, 1), ("S", "P"), ("S", "Q0"), ("S", "z", 2, 0), ("S", "cO"), ("S", "z", 2, 1), ("W", "z", 1, 1),
        ("S", "z", 2, 2), ("S", "z", 1, 0), ("W", "P"), ("S", "P2"), ("S", "z", 1, 2), ("W", "z", 2, 0),
        ("S", "z", 4, 0), ("W", "z", 2, 1), ("S", "Q1"), ("S", "z", 4, 1), ("W", "z", 2, 2), ("S", "z", 3, 2),
        ("W", "Q0"), ("S", "QQ0"), ("S", "z", 4, 2), ("S", "z", 3, 0), ("W", "z", 4, 0), ("S", "z", 6, 0),
        ("W", "P2"), ("W", "z", 4, 1), ("S", "z", 3, 1), ("S", "z", 6, 1), ("S", "cP"), ("S", "QA"), ("W", "z", 3, 2),
        ("W", "z", 4, 2), ("S", "z", 6, 2), ("S", "QB"), ("W", "z", 1, 2), ("W", "Q1"), ("S", "cz", 2), ("S", "cQ1"),
        ("S", "cQ0"), ("W", "z", 6, 0), ("W", "z", 1, 0), ("S", "z", 7, 0), ("S", "QQ1"), ("W", "z", 3, 1),
        ("S", "z", 5, 2), ("S", "z", 5, 0), ("W", "z", 6, 1), ("S", "z", 7, 1), ("S", "cP2"), ("W", "QB"),
        ("W", "QA"), ("W", "z", 6, 2), ("S", "z", 7, 2), ("S", "QQ2"), ("S", "cQ2"), ("S", "cz", 4), ("W", "z", 7, 0),
        ("S", "z", 5, 1), ("S", "cz", 1), ("S", "cz", 6), ("S", "z", 8, 0), ("W", "z", 7, 1), ("S", "z", 8, 1),
        ("W", "QQ1"), ("S", "cz", 3), ("W", "z", 3, 0), ("W", "z", 7, 2), ("S", "z", 8, 2), ("S", "cQQ1"),
        ("S", "cz", 7), ("W", "QQ0"), ("W", "QQ2"), ("W", "z", 5, 1), ("S", "cQQ0"), ("W", "z", 5, 2), ("S", "cz", 5),
        ("W", "z", 8, 1), ("W", "z", 8, 0), ("S", "cQQ2"), ("W", "z", 5, 0), ("W", "z", 8, 2), ("S", "cz", 8),
    ),
)
SENDS = {
    "P": (((0, 0), None, (1, 0)), ((0, 0), None, (-1, 0))),
    "P2": (((-1, 0), 0, (1, 0)), ((1, 0), 1, (-1, 0))),
    "Q0": (((0, 0), None, (0, 1)), ((0, 0), None, (0, -1))),
    "Q1": tuple(((a, 0), None, (0, b)) for a in (-1, 1) for b in (1, -1)),
    "QA": (((2, 0), 0, (0, 1)), ((2, 0), 1, (0, -1))),
    "QB": (((2, 0), 0, (0, -1)), ((2, 0), 1, (0, 1))),
    "QQ0": (((0, -1), 0, (0, 1)), ((0, 1), 1, (0, -1))),
    "QQ1": tuple(((a, -b), (1 - b) // 2, (0, b)) for a in (-1, 1) for b in (1, -1)),
    "QQ2": (((2, -1), 0, (0, 1)), ((2, 1), 1, (0, -1))),
}
NAMES = tuple(SENDS)
BLOCKS = {"P": 2, "P2": 1, "Q0": 2, "Q1": 4, "QA": 1, "QB": 1, "QQ0": 1, "QQ1": 2, "QQ2": 1}
CORE = {
    "cO": ((0, 0),),
    "cP": ((-1, 0), (1, 0)),
    "cP2": ((2, 0),),
    "cQ0": ((0, -1), (0, 1)),
    "cQ1": ((-1, -1), (-1, 1), (1, -1), (1, 1)),
    "cQ2": ((2, -1), (2, 1)),
    "cQQ0": ((0, 2),),
    "cQQ1": ((-1, 2), (1, 2)),
    "cQQ2": ((2, 2),),
}


def kernel(
    ctx_in, res_in, w_in, gain_in, bias_in, tgt_in, probe_in,
    hess_ref, rg_out,
    ctx, stk, pk, wloc, res, tgt, xv, tau, grow, brow, gainb, biasb, mom, mbuf, cbuf, curv, curvt, rg, rs, early, prod, prod0,
    load_sem, ctx_send, g_recv, c_recv, pk_send, pk_recv, w_send, w_recv,
    mom_send, mom_recv, cf_send, cf_recv, rs_send, rs_recv, prod_send, prod_recv,
):
    z = lax.axis_index("dp")
    t = lax.axis_index("tensor")
    core = lax.rem(t, 2)
    x = lax.div(t, 8)
    y = lax.rem(lax.div(t, 2), 4)
    other = t + 1 - 2 * core
    is_one = core == 1
    is_zero = core == 0

    def plane(n):
        return lax.rem(z + n + NZ, NZ)


    def wait_bytes(ref, sem):
        pltpu.make_async_copy(ref, ref, sem).wait()

    def send(src, dst, ssem, rsem, zz, tt):
        pltpu.make_async_remote_copy(
            src_ref=src, dst_ref=dst, send_sem=ssem, recv_sem=rsem, device_id=(zz, tt), device_id_type=MESH
        ).start()

    barrier = pltpu.get_barrier_semaphore()
    for n in (1, -1, 2, -2):
        pl.semaphore_signal(barrier, inc=1, device_id=(plane(n), t), device_id_type=MESH)
    for n in (1, -1):
        pl.semaphore_signal(barrier, inc=1, device_id=(plane(n), other), device_id_type=MESH)

    def greet(i, carry):
        pl.semaphore_signal(barrier, inc=1, device_id=(z, lax.rem(t + i, NT)), device_id_type=MESH)
        return carry

    lax.fori_loop(1, NT, greet, 0)

    own_rows = pl.ds(pl.multiple_of(t * BLK, 32), BLK)
    own = ctx.at[own_rows, :]
    loads = [
        pltpu.make_async_copy(w_in, wloc, load_sem.at[0]),
        pltpu.make_async_copy(probe_in, stk.at[pl.ds(ROWS, ROWS), :], load_sem.at[1]),
        pltpu.make_async_copy(ctx_in, own, load_sem.at[2]),
        pltpu.make_async_copy(res_in, res, load_sem.at[3]),
        pltpu.make_async_copy(tgt_in, tgt, load_sem.at[4]),
        pltpu.make_async_copy(gain_in, grow, load_sem.at[6]),
        pltpu.make_async_copy(bias_in, brow, load_sem.at[7]),
    ]
    for c in loads:
        c.start()
    loads[0].wait()
    half_at = pl.multiple_of((1 - core) * PK, 32)
    pk[z, pl.ds(half_at, 192), :] = wloc[:, 0:128]
    pk[z, pl.ds(half_at + 192, 96), 0:64] = wloc[0:96, 128:192]
    pk[z, pl.ds(half_at + 192, 96), 64:128] = wloc[96:192, 128:192]
    pl.semaphore_wait(barrier, NT + 5)

    def zero_half(j):
        return pk.at[j, pl.ds(PK, PK), :]

    def pk_sub(j, s):
        return pk.at[j, pl.ds(s * ZSUB, ZSUB), :]

    def gather(c):
        p, q = (y, x) if c else (x, y)
        sp, sq = (2, 8) if c else (8, 2)

        def dev(dp, dq):
            return lax.rem(p + dp + 4, 4) * sp + lax.rem(q + dq + 4, 4) * sq + c

        def rows_of(dp, dq):
            return pl.ds(pl.multiple_of(dev(dp, dq) * BLK, 32), BLK)

        def blk(dp, dq, half=None):
            rows = rows_of(dp, dq)
            return ctx.at[rows, :] if half is None else ctx.at[rows, pl.ds(half * 512, 512)]

        if c == 0:
            send(zero_half(z), zero_half(z), w_send, w_recv, z, other)
        waited = False
        for act, name, *ab in PLAN[c]:
            if name == "cz":
                for sign in (1, -1)[: 1 if ab[0] == 8 else 2]:
                    ref = zero_half(plane(sign * ab[0]))
                    send(ref, ref, w_send, w_recv, z, other)
            elif name in CORE:
                for at in CORE[name]:
                    src = ctx_in if name == "cO" else blk(*at)
                    send(src, blk(*at), ctx_send, c_recv, z, other)
            elif name == "z":
                n, part = ab
                sem = pk_recv.at[(n - 1) * 3 + part]
                signs = (1, -1) if n < 8 else (1,) if part < 2 else (-1,)
                if act == "W":
                    wait_bytes(pk.at[pl.ds(0, len(signs)), pl.ds(0, ZSUB), :], sem)
                    continue
                hop = 2 if n <= FAST and n % 2 == 0 else 1
                if n == hop and not waited:
                    waited = True
                    wait_bytes(zero_half(z), w_recv)
                for sign in signs:
                    ref = pk_sub(plane(sign * (hop - n)), part)
                    send(ref, ref, pk_send, sem, plane(sign * hop), t)
            elif act == "S":
                for at, half, to in SENDS[name]:
                    dst = blk(*at, half)
                    send(ctx_in if at == (0, 0) else dst, dst, ctx_send, g_recv.at[NAMES.index(name)], z, dev(*to))
            else:
                wait_bytes(ctx.at[pl.ds(0, BLOCKS[name] * BLK), :], g_recv.at[NAMES.index(name)])
        if c == 0:
            wait_bytes(pk.at[pl.ds(0, NZ - 1), pl.ds(0, PK), :], w_recv)

    @pl.when(is_zero)
    def _():
        gather(0)

    @pl.when(is_one)
    def _():
        gather(1)

    for c in loads[5:]:
        c.wait()
    gainb[...] = jnp.transpose(jnp.broadcast_to(grow[...], (128, ROWS)))
    biasb[...] = jnp.transpose(jnp.broadcast_to(brow[...], (128, ROWS)))
    for j in range(NZ):
        c = 192 * j
        stk[0:192, c : c + 128] = pk[j, pl.ds(half_at, 192), :]
        stk[0:96, c + 128 : c + 192] = pk[j, pl.ds(half_at + 192, 96), 0:64]
        stk[96:192, c + 128 : c + 192] = pk[j, pl.ds(half_at + 192, 96), 64:128]
    wait_bytes(ctx.at[pl.ds(0, 16 * BLK), :], c_recv)
    for c in loads[1:5]:
        c.wait()

    for n in range(2):
        cols = slice(n * 512, (n + 1) * 512)
        both = jnp.dot(stk[...], ctx[:, cols], preferred_element_type=F32)
        xv[:, cols] = both[0:192]
        tau[:, cols] = both[192:384]

    def sums(i, carry):
        k = lax.rem(2 * x + 4 + i, 8)
        lanes = pl.ds(pl.multiple_of(k * 128, 128), 128)
        tot = jnp.zeros((16, 128), F32)
        for r in range(12):
            rows = pl.ds(r * 16, 16)
            xx = xv[rows, lanes] + res[rows, lanes].astype(F32)
            xv[rows, lanes] = xx
            tot = tot + xx
        mean = jnp.sum(tot, axis=0, keepdims=True) / ROWS
        accs = [jnp.zeros((16, 128), F32) for _ in range(11)]
        for r in range(12):
            rows = pl.ds(r * 16, 16)
            yy = xv[rows, lanes] - mean
            tt = tau[rows, lanes]
            g = gainb[rows, :]
            w = g * g
            h = g * (biasb[rows, :] - tgt[rows, lanes].astype(F32))
            wy = w * yy
            wt = w * tt
            terms = (yy * yy, wy, wy * yy, h, h * yy, tt, yy * tt, wt, wy * tt, h * tt, w)
            accs = [a + b for a, b in zip(accs, terms)]
        mom[k, 0:1, :] = mean
        for a in range(11):
            mom[k, a + 1 : a + 2, :] = jnp.sum(accs[a], axis=0, keepdims=True)
        mom[k, 12:16, :] = jnp.ones((4, 128), F32)

        @pl.when(t != 4 * k + 1)
        def _():
            send(mom.at[k], mbuf.at[t], mom_send, mom_recv, z, 4 * k + 1)

        return carry

    lax.fori_loop(0, 8, sums, 0)
    mine = lax.div(t, 4)
    is_owner = lax.rem(t, 4) == 1

    @pl.when(is_owner)
    def _():
        mbuf[t] = mom[mine]
        wait_bytes(mbuf.at[pl.ds(0, NT - 1)], mom_recv)
        s0 = mbuf[0]
        for i in range(1, NT):
            s0 = s0 + mbuf[i]
        mean = s0[0:1] / NT
        s1 = jnp.zeros((16, 128), F32)
        s2 = jnp.zeros((16, 128), F32)
        for i in range(NT):
            m = mbuf[i]
            dm = (m[0:1] - mean) * m
            s1 = s1 + dm
            s2 = s2 + (m[0:1] - mean) * dm

        def row(a, i):
            return a[i : i + 1]

        s_w = row(s0, 11)
        s_h = row(s0, 4)
        s_t = row(s0, 6)
        s_wt = row(s0, 8)
        s_ht = row(s0, 10)
        s_zz = row(s0, 1) + ROWS * row(s2, 12)
        s_wz = row(s0, 2) + row(s1, 11)
        s_wzz = row(s0, 3) + 2 * row(s1, 2) + row(s2, 11)
        s_hz = row(s0, 5) + row(s1, 4)
        s_zt = row(s0, 7) + row(s1, 6)
        s_wzt = row(s0, 9) + row(s1, 8)
        sc = 1.0 / jnp.sqrt(s_zz / D + 1e-05)
        s_wn = sc * s_wz
        s_wnn = sc * sc * s_wzz
        s_hn = sc * s_hz
        g_mean = (s_wn + s_h) / D
        g_proj = (s_wnn + s_hn) / D
        t_mean = s_t / D
        t_proj = sc * s_zt / D
        c_mean = sc * (s_wt - t_mean * s_w - t_proj * s_wn) / D
        c_proj = sc * (2 * (sc * s_wzt - t_mean * s_wn - t_proj * s_wnn) + s_ht - t_mean * s_h - t_proj * s_hn) / D
        for i, v in enumerate((mean, sc, g_mean, g_proj, t_mean, t_proj, c_mean, c_proj)):
            cbuf[mine, i : i + 1, :] = v

        steps = sorted(((dx, dy) for dx in range(4) for dy in range(4)), key=lambda d: -min(d[0], 4 - d[0]) - min(d[1], 4 - d[1]))
        for dx, dy in steps:
            chip = lax.rem(x + dx, 4) * 8 + lax.rem(y + dy, 4) * 2
            for c in (0, 1):
                if (dx, dy, c) != (0, 0, 1):
                    send(cbuf.at[mine], cbuf.at[mine], cf_send, cf_recv.at[mine], z, chip + c)

    def finish(i, carry):
        k = lax.rem(2 * x + 6 + i, 8)

        @pl.when(t != 4 * k + 1)
        def _():
            wait_bytes(cbuf.at[k], cf_recv.at[k])

        lanes = pl.ds(pl.multiple_of(k * 128, 128), 128)
        mean, sc, g_mean, g_proj, t_mean, t_proj, c_mean, c_proj = [cbuf[k, a : a + 1, :] for a in range(8)]
        lead = -sc * t_proj
        for r in range(12):
            rows = pl.ds(r * 16, 16)
            n = (xv[rows, lanes] - mean) * sc
            g = gainb[rows, :]
            w = g * g
            gn = g * (g * n + biasb[rows, :] - tgt[rows, lanes].astype(F32))
            grad = sc * (gn - g_mean - n * g_proj)
            rg[rows, lanes] = grad
            u = sc * (tau[rows, lanes] - t_mean - n * t_proj)
            cv = lead * grad + sc * (w * u - c_mean - u * g_proj - n * c_proj)
            curv[rows, :] = cv
            if r >= 8:
                curv[pl.ds(r * 16 + 64, 16), :] = cv
        curvt[pl.ds(pl.multiple_of(k * 128, 128), 128), :] = jnp.transpose(curv[...]).astype(BF16)
        return carry

    lax.fori_loop(0, 8, finish, 0)
    rg_copy = pltpu.make_async_copy(rg, rg_out, load_sem.at[5])
    rg_copy.start()

    lane = lax.broadcasted_iota(jnp.int32, (96, 128), 1)

    def pack(full, to, slot):
        to[slot, 0:192, :] = full[:, 0:128]
        to[slot, 192:288, :] = jnp.where(lane < 64, full[0:96, 128:256], full[96:192, 128:256])

    def product(i, to, slot):
        rows = pl.ds(pl.multiple_of(wanted(i) * 192, 64), 192)
        pack(jnp.dot(ctx[rows, :], curvt[...], preferred_element_type=F32), to, slot)

    def products():
        for b in range(4):
            full = jnp.dot(ctx[768 * b : 768 * (b + 1), :], curvt[...], preferred_element_type=F32)
            for i in range(4):
                pack(full[192 * i : 192 * (i + 1)], prod, 4 * b + i)

    def wanted(i):
        return plane(8 + (1 - 2 * lax.rem(i, 2)) * lax.div(i + 1, 2))

    def finish_hess(both):
        pair = stk[192:384, pl.ds(pl.multiple_of(lax.div(z, 2) * 384, 128), 384)].astype(F32)
        pc = jnp.where(lax.rem(z, 2) == 0, pair[:, 0:192], pair[:, 192:384]) * (1.0 / TOKENS)
        at = jnp.transpose(both[0:192])
        bt = jnp.transpose(both[192:288])
        hess_ref[0:128, :] = pc[0:128] * at
        hess_ref[128:192, 0:96] = pc[128:192, 0:96] * bt[0:64]
        hess_ref[128:192, 96:192] = pc[128:192, 96:192] * bt[64:128]

    def rs_sub(w, n, s):
        return rs.at[(w * 9 + n) * 4 + s]

    def rs_sem(w, n, s):
        return rs_recv.at[(w * 8 + n - 1) * 4 + s]

    def rs_take(w, n, s):
        wait_bytes(rs_sub(w, n, s), rs_sem(w, n, s))

    def decode(w, n, s):
        at = (w * 9 + n) * 4 + s
        near = rs[at, 0:RSUB, :].astype(F32)
        low = rs[at, RSUB:RMSG, :].astype(F32)
        one = jnp.round(low * (1 / 21))
        two = low - 21 * one
        steps = jnp.concatenate([one, two[0:64]], axis=0)
        return near + near * (steps * LOW)

    def last_of(first):
        parts = []
        for s in (first, first + 1):
            for w in range(2):
                rs_take(w, 8, s)
            parts.append(decode(0, 8, s) + decode(1, 8, s))
        finish_hess(prod[z] + jnp.concatenate(parts, axis=0))

    @pl.when(is_zero)
    def _():
        for group, (lo, hi) in enumerate(GROUPS):

            def hand(i, carry, group=group):
                product(i, prod, wanted(i))
                send(prod.at[wanted(i)], prod0.at[i], prod_send, prod_recv.at[group], z, other)
                return carry

            lax.fori_loop(lo, hi, hand, 0)
        product(NZ - 1, prod, z)
        last_of(2)
        wait_bytes(prod.at[pl.ds(0, NZ - 1)], prod_send)

    @pl.when(is_one)
    def _():
        def rs_pass(w, n, s):
            to = other if n == 7 and s > 1 else t
            send(rs_sub(w, n, s), rs_sub(w, n + 1, s), rs_send, rs_sem(w, n + 1, s), plane(1 - 2 * w), to)

        def own(i, s):
            lo = s % 2 * RSUB
            if s > 1:
                return prod0[i, lo : lo + RSUB, :]
            return early[i // 2, lo : lo + RSUB, :] if i in (0, 2) else prod[wanted(i), lo : lo + RSUB, :]

        def code(w, n, s, v):
            at = (w * 9 + n) * 4 + s
            high = v.astype(BF16)
            near = high.astype(F32)
            rest = jnp.where(jnp.abs(near) > 1e-30, (v - near) * pl.reciprocal(near, approx=True), 0.0)
            steps = jnp.round(rest * (1 / LOW))
            rs[at, 0:RSUB, :] = high
            rs[at, RSUB : RSUB + 64, :] = (21 * steps[0:64] + steps[80:RSUB]).astype(BF16)
            rs[at, RSUB + 64 : RMSG, :] = (21 * steps[64:80]).astype(BF16)

        def put(w, n, i, s, add):
            v = own(i, s)
            if add:
                rs_take(w, n, s)
                v = v + decode(w, n, s)
            code(w, n, s, v)
            rs_pass(w, n, s)

        def theirs(group):
            lo, hi = GROUPS[group]
            wait_bytes(prod0.at[pl.ds(lo, hi - lo)], prod_recv.at[group])

        product(0, early, 0)
        for s in (0, 1):
            put(0, 0, 0, s, False)
        theirs(0)
        for s in (2, 3):
            put(1, 0, 0, s, False)
        product(2, early, 1)
        for s in (0, 1):
            put(1, 1, 2, s, False)
        theirs(1)
        for s in (2, 3):
            put(0, 1, 1, s, False)
        products()
        theirs(2)
        for s in (0, 1):
            put(0, 1, 1, s, True)
            put(1, 1, 2, s + 2, True)
        for n in range(2, 8):
            if n < 5:
                theirs(n + 1)
            for s in (2, 3, 0, 1):
                put(0, n, 2 * n - 1, s, True)
                put(1, n, 2 * n, s ^ 2, True)
        last_of(0)
        wait_bytes(rs.at[pl.ds(0, 60)], rs_send)
        wait_bytes(pk.at[pl.ds(0, 15)], pk_send)
        wait_bytes(pk.at[pl.ds(0, 15), pl.ds(0, PK), :], w_send)

    rg_copy.wait()
    wait_bytes(ctx.at[pl.ds(0, 31 * BLK), :], ctx_send)

    @pl.when(is_zero)
    def _():
        wait_bytes(pk.at[0, pl.ds(0, PK), :], w_send)

    @pl.when(is_owner)
    def _():
        wait_bytes(mom.at[pl.ds(0, 7)], mom_send)
        wait_bytes(prod.at[0, pl.ds(0, 8 * (NT - 1)), :], cf_send)

    @pl.when(jnp.logical_not(is_owner))
    def _():
        wait_bytes(mom, mom_send)


def shards(context, residual, out_weight, norm_gain, norm_bias, target, probe):
    hbm = pl.BlockSpec(memory_space=pltpu.HBM)
    anywhere = pl.BlockSpec(memory_space=pl.ANY)
    vmem = pl.BlockSpec(memory_space=pltpu.VMEM)
    dma = pltpu.SemaphoreType.DMA
    arrays = (context, residual, out_weight, norm_gain.reshape(1, ROWS), norm_bias.reshape(1, ROWS), target, probe)
    arrays = [pltpu.with_memory_space_constraint(a, pltpu.HBM) for a in arrays]
    return pl.pallas_call(
        kernel,
        out_shape=(
            jax.ShapeDtypeStruct((ROWS, 192), F32),
            jax.ShapeDtypeStruct((ROWS, TOK), F32),
        ),
        in_specs=[hbm] * 7,
        out_specs=(vmem, anywhere),
        scratch_shapes=[
            pltpu.VMEM((NT * BLK, TOK), BF16),
            pltpu.VMEM((2 * ROWS, 3072), BF16),
            pltpu.VMEM((NZ, 2 * PK, 128), BF16),
            pltpu.VMEM((192, 192), BF16),
            pltpu.VMEM((ROWS, TOK), BF16),
            pltpu.VMEM((ROWS, TOK), BF16),
            pltpu.VMEM((ROWS, TOK), F32),
            pltpu.VMEM((ROWS, TOK), F32),
            pltpu.VMEM((1, ROWS), F32),
            pltpu.VMEM((1, ROWS), F32),
            pltpu.VMEM((ROWS, 128), F32),
            pltpu.VMEM((ROWS, 128), F32),
            pltpu.VMEM((8, 16, 128), F32),
            pltpu.VMEM((NT, 16, 128), F32),
            pltpu.VMEM((8, 8, 128), F32),
            pltpu.VMEM((256, 128), F32),
            pltpu.VMEM((TOK, 256), BF16),
            pltpu.VMEM((ROWS, TOK), F32),
            pltpu.VMEM((18 * 4, RMSG, 128), BF16),
            pltpu.VMEM((2, PK, 128), F32),
            pltpu.VMEM((NZ, PK, 128), F32),
            pltpu.VMEM((NZ, PK, 128), F32),
            dma((8,)),
            dma,
            dma((9,)),
            dma,
            dma,
            dma((24,)),
            dma,
            dma,
            dma,
            dma,
            dma,
            dma((8,)),
            dma,
            dma((64,)),
            dma,
            dma((len(GROUPS),)),
        ],
        compiler_params=pltpu.CompilerParams(
            collective_id=0, has_side_effects=True, vmem_limit_bytes=48 * 1024 * 1024
        ),
    )(*arrays)


def solution(mesh):
    return jax.shard_map(
        shards,
        mesh=mesh,
        in_specs=(
            P("tensor", "dp"),
            P("tensor", "dp"),
            P("tensor", "dp"),
            P("tensor"),
            P("tensor"),
            P("tensor", "dp"),
            P("tensor", None),
        ),
        out_specs=(P("tensor", "dp"), P("tensor", "dp")),
        check_vma=False,
    )
```

time: 84.4 us -> 80.4 us (0.953)
  Pallas kernels: 82 us -> 78.1 us
    pallas_call x1, Pallas kernels: 82 us -> 78.1 us  [shards(): pl.pallas_call(kernel, out_shape=(jax.ShapeDtypeStruct((ROWS, 192), F32),...]
where the time goes in v4:
time: 80.4 us; the launch traced here: 80.3 us
  Pallas kernels  78.1 us (97%)
  local copies, waits for them, and re-layouts  1.56 us (2%)
    pallas_call x1, Pallas kernels, shards(): pl.pallas_call(kernel, out_shape=(jax.ShapeDtypeStruct((ROWS, 192), F32),...  78.1 us

profile of v4, /device:TPU:1, one launch (start us, length us, event | category | flops | bytes accessed | tf_op | source)
XLA Modules:
  0.0 80.3 jit_solution(3507852366494896496)
XLA Ops:
  0.6 78.1 %shard_map.86 = (f32[192,192]{1,0:T(8,128)S(1)}, f32[192,1024]{1,0:T(8,128)S(1)}) custom-call(bf16[96,1024]{1,0:T(8,128)(2,1)} %ctx_in.1, bf16[192,1024]{1,0:T(8,128)(2,1)} %res_in.1, bf16[192,192]{1,0:T(8,128)(2,1)} %w_in.1, f32[1,192]{1,0:T(1,128)} %bitcast.2, f32[1,192]{1,0:T(1,128)} %bitcast.3, bf16[192,1024]{1,0:T(8,128)(2,1)} %tgt_in.1, ...), custom_call_target="tpu_custom_call" | custom-call | tf_op jit(solution)/shard_map/pallas_call | solution.py:489
  78.7 0.7 copy.11
  79.4 0.9 %copy.12 = f32[192,1024]{1,0:T(8,128)} copy(f32[192,1024]{1,0:T(8,128)S(1)} %get-tuple-element.5) | data formatting | bytes 1572864

commit v5 on v4

--- a/solution.py
+++ b/solution.py
@@ -26,25 +26,26 @@
 
 PLAN = (
     (
-        ("S", "Q0"), ("S", "P"), ("W", "P"), ("W", "Q0"), ("S", "QQ0"), ("S", "cP"), ("S", "Q1"), ("S", "P2"),
-        ("W", "QQ0"), ("W", "P2"), ("S", "cQ0"), ("S", "QA"), ("S", "QB"), ("W", "Q1"), ("S", "QQ1"), ("W", "QA"),
-        ("S", "cP2"), ("S", "QQ2"), ("S", "cQQ0"), ("W", "QB"), ("S", "cQ1"), ("S", "cQ2"), ("W", "QQ1"),
-        ("S", "cQQ1"), ("W", "QQ2"), ("S", "cQQ2"), ("S", "cO"),
+        ("S", "cO"), ("S", "P"), ("S", "Q0"), ("W", "P"), ("S", "Q1"), ("S", "P2"), ("W", "P2"), ("S", "QA"),
+        ("S", "cP2"), ("S", "cP"), ("W", "Q0"), ("S", "QQ0"), ("S", "QB"), ("W", "Q1"), ("S", "QQ1"), ("S", "cQ0"),
+        ("W", "QA"), ("S", "QQ2"), ("S", "cQ1"), ("W", "QB"), ("W", "QQ0"), ("S", "cQ2"), ("W", "QQ1"), ("S", "cQQ1"),
+        ("S", "cQQ0"), ("W", "QQ2"), ("S", "cQQ2"),
     ),
     (
-        ("S", "z", 1, 1), ("S", "P"), ("S", "Q0"), ("S", "z", 2, 0), ("S", "cO"), ("S", "z", 2, 1), ("W", "z", 1, 1),
-        ("S", "z", 2, 2), ("S", "z", 1, 0), ("W", "P"), ("S", "P2"), ("S", "z", 1, 2), ("W", "z", 2, 0),
-        ("S", "z", 4, 0), ("W", "z", 2, 1), ("S", "Q1"), ("S", "z", 4, 1), ("W", "z", 2, 2), ("S", "z", 3, 2),
-        ("W", "Q0"), ("S", "QQ0"), ("S", "z", 4, 2), ("S", "z", 3, 0), ("W", "z", 4, 0), ("S", "z", 6, 0),
-        ("W", "P2"), ("W", "z", 4, 1), ("S", "z", 3, 1), ("S", "z", 6, 1), ("S", "cP"), ("S", "QA"), ("W", "z", 3, 2),
-        ("W", "z", 4, 2), ("S", "z", 6, 2), ("S", "QB"), ("W", "z", 1, 2), ("W", "Q1"), ("S", "cz", 2), ("S", "cQ1"),
-        ("S", "cQ0"), ("W", "z", 6, 0), ("W", "z", 1, 0), ("S", "z", 7, 0), ("S", "QQ1"), ("W", "z", 3, 1),
-        ("S", "z", 5, 2), ("S", "z", 5, 0), ("W", "z", 6, 1), ("S", "z", 7, 1), ("S", "cP2"), ("W", "QB"),
-        ("W", "QA"), ("W", "z", 6, 2), ("S", "z", 7, 2), ("S", "QQ2"), ("S", "cQ2"), ("S", "cz", 4), ("W", "z", 7, 0),
-        ("S", "z", 5, 1), ("S", "cz", 1), ("S", "cz", 6), ("S", "z", 8, 0), ("W", "z", 7, 1), ("S", "z", 8, 1),
-        ("W", "QQ1"), ("S", "cz", 3), ("W", "z", 3, 0), ("W", "z", 7, 2), ("S", "z", 8, 2), ("S", "cQQ1"),
-        ("S", "cz", 7), ("W", "QQ0"), ("W", "QQ2"), ("W", "z", 5, 1), ("S", "cQQ0"), ("W", "z", 5, 2), ("S", "cz", 5),
-        ("W", "z", 8, 1), ("W", "z", 8, 0), ("S", "cQQ2"), ("W", "z", 5, 0), ("W", "z", 8, 2), ("S", "cz", 8),
+        ("S", "P"), ("S", "z", 2, 0), ("S", "z", 2, 1), ("S", "cO"), ("S", "z", 2, 2), ("S", "z", 1, 2),
+        ("W", "z", 2, 0), ("S", "Q0"), ("S", "z", 4, 0), ("W", "z", 1, 2), ("S", "z", 1, 1), ("S", "z", 1, 0),
+        ("W", "P"), ("S", "P2"), ("W", "z", 2, 1), ("S", "z", 4, 1), ("W", "z", 2, 2), ("S", "Q1"), ("W", "z", 4, 0),
+        ("S", "z", 4, 2), ("W", "z", 1, 0), ("S", "z", 3, 2), ("S", "z", 6, 0), ("W", "z", 1, 1), ("W", "z", 4, 1),
+        ("S", "cz", 2), ("S", "z", 6, 1), ("W", "Q0"), ("S", "cP"), ("W", "P2"), ("S", "z", 3, 1), ("S", "QA"),
+        ("W", "z", 4, 2), ("S", "z", 6, 2), ("S", "cP2"), ("S", "QB"), ("W", "z", 6, 0), ("S", "QQ0"),
+        ("S", "z", 7, 0), ("S", "cz", 4), ("W", "Q1"), ("S", "z", 5, 1), ("S", "cQ1"), ("W", "z", 6, 1),
+        ("S", "z", 7, 1), ("S", "QQ1"), ("S", "cQ0"), ("S", "z", 5, 0), ("W", "z", 3, 1), ("W", "z", 6, 2),
+        ("S", "z", 7, 2), ("S", "cz", 1), ("W", "QB"), ("W", "QA"), ("W", "z", 5, 1), ("S", "z", 3, 0),
+        ("S", "z", 5, 2), ("S", "cQ2"), ("W", "z", 3, 2), ("W", "z", 7, 1), ("S", "cz", 6), ("S", "QQ2"),
+        ("S", "cz", 3), ("W", "z", 7, 0), ("S", "z", 8, 1), ("W", "z", 5, 0), ("W", "QQ0"), ("W", "z", 7, 2),
+        ("S", "z", 8, 2), ("S", "cQQ0"), ("S", "cz", 7), ("W", "QQ1"), ("S", "z", 8, 0), ("S", "cQQ1"),
+        ("W", "z", 5, 2), ("S", "cz", 5), ("W", "z", 8, 1), ("W", "QQ2"), ("S", "cQQ2"), ("W", "z", 8, 2),
+        ("S", "cz", 8), ("W", "z", 3, 0), ("W", "z", 8, 0),
     ),
 )
 SENDS = {
@@ -126,12 +127,15 @@
     ]
     for c in loads:
         c.start()
-    loads[0].wait()
+    pl.semaphore_wait(barrier, NT + 5)
+
     half_at = pl.multiple_of((1 - core) * PK, 32)
-    pk[z, pl.ds(half_at, 192), :] = wloc[:, 0:128]
-    pk[z, pl.ds(half_at + 192, 96), 0:64] = wloc[0:96, 128:192]
-    pk[z, pl.ds(half_at + 192, 96), 64:128] = wloc[96:192, 128:192]
-    pl.semaphore_wait(barrier, NT + 5)
+
+    def pack_weight():
+        loads[0].wait()
+        pk[z, pl.ds(half_at, 192), :] = wloc[:, 0:128]
+        pk[z, pl.ds(half_at + 192, 96), 0:64] = wloc[0:96, 128:192]
+        pk[z, pl.ds(half_at + 192, 96), 64:128] = wloc[96:192, 128:192]
 
     def zero_half(j):
         return pk.at[j, pl.ds(PK, PK), :]
@@ -153,10 +157,13 @@
             rows = rows_of(dp, dq)
             return ctx.at[rows, :] if half is None else ctx.at[rows, pl.ds(half * 512, 512)]
 
-        if c == 0:
-            send(zero_half(z), zero_half(z), w_send, w_recv, z, other)
-        waited = False
+        packed = waited = False
         for act, name, *ab in PLAN[c]:
+            if not packed and (act == "W" or name == "z"):
+                packed = True
+                pack_weight()
+                if c == 0:
+                    send(zero_half(z), zero_half(z), w_send, w_recv, z, other)
             if name == "cz":
                 for sign in (1, -1)[: 1 if ab[0] == 8 else 2]:
                     ref = zero_half(plane(sign * ab[0]))
@@ -173,7 +180,7 @@
                     wait_bytes(pk.at[pl.ds(0, len(signs)), pl.ds(0, ZSUB), :], sem)
                     continue
                 hop = 2 if n <= FAST and n % 2 == 0 else 1
-                if n == hop and not waited:
+                if n == hop and part > 0 and not waited:
                     waited = True
                     wait_bytes(zero_half(z), w_recv)
                 for sign in signs:

time: 80.4 us -> 78.7 us (0.979)
  Pallas kernels: 78.1 us -> 76.4 us
    pallas_call x1, Pallas kernels: 78.1 us -> 76.4 us  [shards(): pl.pallas_call(kernel, out_shape=(jax.ShapeDtypeStruct((ROWS, 192), F32),...]
where the time goes in v5:
time: 78.7 us; the launch traced here: 78.6 us
  Pallas kernels  76.4 us (97%)
  local copies, waits for them, and re-layouts  1.56 us (2%)
    pallas_call x1, Pallas kernels, shards(): pl.pallas_call(kernel, out_shape=(jax.ShapeDtypeStruct((ROWS, 192), F32),...  76.4 us

profile of v5, /device:TPU:1, one launch (start us, length us, event | category | flops | bytes accessed | tf_op | source)
XLA Modules:
  0.0 78.6 jit_solution(319215157183912114)
XLA Ops:
  0.6 76.4 %shard_map.86 = (f32[192,192]{1,0:T(8,128)S(1)}, f32[192,1024]{1,0:T(8,128)S(1)}) custom-call(bf16[96,1024]{1,0:T(8,128)(2,1)} %ctx_in.1, bf16[192,1024]{1,0:T(8,128)(2,1)} %res_in.1, bf16[192,192]{1,0:T(8,128)(2,1)} %w_in.1, f32[1,192]{1,0:T(1,128)} %bitcast.2, f32[1,192]{1,0:T(1,128)} %bitcast.3, bf16[192,1024]{1,0:T(8,128)(2,1)} %tgt_in.1, ...), custom_call_target="tpu_custom_call" | custom-call | tf_op jit(solution)/shard_map/pallas_call | solution.py:496
  77.0 0.7 copy.11
  77.7 0.9 %copy.12 = f32[192,1024]{1,0:T(8,128)} copy(f32[192,1024]{1,0:T(8,128)S(1)} %get-tuple-element.5) | data formatting | bytes 1572864

commit v6 on v5

--- a/solution.py
+++ b/solution.py
@@ -102,6 +102,8 @@
             src_ref=src, dst_ref=dst, send_sem=ssem, recv_sem=rsem, device_id=(zz, tt), device_id_type=MESH
         ).start()
 
+    weight_load = pltpu.make_async_copy(w_in, wloc, load_sem.at[0])
+    weight_load.start()
     barrier = pltpu.get_barrier_semaphore()
     for n in (1, -1, 2, -2):
         pl.semaphore_signal(barrier, inc=1, device_id=(plane(n), t), device_id_type=MESH)
@@ -117,7 +119,7 @@
     own_rows = pl.ds(pl.multiple_of(t * BLK, 32), BLK)
     own = ctx.at[own_rows, :]
     loads = [
-        pltpu.make_async_copy(w_in, wloc, load_sem.at[0]),
+        weight_load,
         pltpu.make_async_copy(probe_in, stk.at[pl.ds(ROWS, ROWS), :], load_sem.at[1]),
         pltpu.make_async_copy(ctx_in, own, load_sem.at[2]),
         pltpu.make_async_copy(res_in, res, load_sem.at[3]),
@@ -125,7 +127,7 @@
         pltpu.make_async_copy(gain_in, grow, load_sem.at[6]),
         pltpu.make_async_copy(bias_in, brow, load_sem.at[7]),
     ]
-    for c in loads:
+    for c in loads[1:]:
         c.start()
     pl.semaphore_wait(barrier, NT + 5)
 
@@ -337,7 +339,6 @@
 
     lax.fori_loop(0, 8, finish, 0)
     rg_copy = pltpu.make_async_copy(rg, rg_out, load_sem.at[5])
-    rg_copy.start()
 
     lane = lax.broadcasted_iota(jnp.int32, (96, 128), 1)
 
@@ -404,6 +405,7 @@
 
             lax.fori_loop(lo, hi, hand, 0)
         product(NZ - 1, prod, z)
+        rg_copy.start()
         last_of(2)
         wait_bytes(prod.at[pl.ds(0, NZ - 1)], prod_send)
 
@@ -453,6 +455,7 @@
         theirs(1)
         for s in (2, 3):
             put(0, 1, 1, s, False)
+        rg_copy.start()
         products()
         theirs(2)
         for s in (0, 1):

time: 78.7 us -> 78.7 us (level)
  no operation moved by 1% of the time
where the time goes in v6:
time: 78.7 us; the launch traced here: 78.6 us
  Pallas kernels  76.4 us (97%)
  local copies, waits for them, and re-layouts  1.56 us (2%)
    pallas_call x1, Pallas kernels, shards(): pl.pallas_call(kernel, out_shape=(jax.ShapeDtypeStruct((ROWS, 192), F32),...  76.4 us

profile of v6, /device:TPU:1, one launch (start us, length us, event | category | flops | bytes accessed | tf_op | source)
XLA Modules:
  0.0 78.6 jit_solution(3910957643407927232)
XLA Ops:
  0.6 76.4 %shard_map.86 = (f32[192,192]{1,0:T(8,128)S(1)}, f32[192,1024]{1,0:T(8,128)S(1)}) custom-call(bf16[96,1024]{1,0:T(8,128)(2,1)} %ctx_in.1, bf16[192,1024]{1,0:T(8,128)(2,1)} %res_in.1, bf16[192,192]{1,0:T(8,128)(2,1)} %w_in.1, f32[1,192]{1,0:T(1,128)} %bitcast.2, f32[1,192]{1,0:T(1,128)} %bitcast.3, bf16[192,1024]{1,0:T(8,128)(2,1)} %tgt_in.1, ...), custom_call_target="tpu_custom_call" | custom-call | tf_op jit(solution)/shard_map/pallas_call | solution.py:499
  77.0 0.7 copy.11
  77.7 0.9 %copy.12 = f32[192,1024]{1,0:T(8,128)} copy(f32[192,1024]{1,0:T(8,128)S(1)} %get-tuple-element.5) | data formatting | bytes 1572864
